TPU v7x, 32 devices: a whole 2x2x4 slice. The times are simulated.
32 devices in a mesh: groups: 2 (over y), dp: 4 (over z), fsdp: 4 (over x, core).
Axes of the slice: x: 2, y: 2, z: 4, core: 2. Of those that a mesh axis runs over, the one named last changes fastest.
Arguments:
- activations: bfloat16 [6144, 28672], P(('groups', 'dp'), 'fsdp'), parts along dimension 0, may hold values from -6 to 6
- out_grad: bfloat16 [6144, 8192], P(('groups', 'dp'), 'fsdp'), parts along dimension 0, may hold values from -0.0059814453 to 0.0059814453
- basis: bfloat16 [16384, 128], P('groups'), parts along dimension 0, may hold values from -0.5 to 0.5
- first_moment: float32 [57344, 128], P(('groups', 'fsdp', 'dp')), parts along dimension 0, may hold values from -0.6 to 0.6
- second_moment: float32 [57344, 128], P(('groups', 'fsdp', 'dp')), parts along dimension 0, may hold values from 0.0001 to 0.001
Outputs:
- update: bfloat16 [57344, 8192], P(('groups', 'fsdp'), 'dp'), parts along dimension 0
- first_next: float32 [57344, 128], P(('groups', 'fsdp', 'dp')), parts along dimension 0
- second_next: float32 [57344, 128], P(('groups', 'fsdp', 'dp')), parts along dimension 0
There are 2 independent parts, one for each index of `groups`. A program takes and returns all parts, laid end to end along the dimension named above; each array names one. Nothing has to cross between parts.
All inputs are finite; a program needn't handle non-finite values.
Results may differ from a plain program's by a relative error of at most 0.0049.
The roundings to bfloat16 on the way count: a program that leaves them out, or rounds other values in their place, can miss the bound.
Values may be sent and summed in bfloat16 or wider, within the bound.
No kernel may reach another device: no remote copies, remote signals or barrier semaphores. Data moves between devices by JAX's collectives and lax.ppermute only.
A program may use at most 128 MiB of HBM per device.

v0:
```python
import jax
import jax.numpy as jnp
from jax import lax
from jax.sharding import PartitionSpec as P

STEP = 10


def on_device(activations, out_grad, basis, first_moment, second_moment):
    features = out_grad.shape[1]
    fsdp_index = lax.axis_index("fsdp")
    basis_rows = lax.dynamic_slice_in_dim(basis, fsdp_index * features, features, 0)
    partial_proj = jnp.dot(out_grad, basis_rows, preferred_element_type=jnp.float32)
    projected = lax.psum(partial_proj, "fsdp").astype(jnp.bfloat16)
    low_grad = lax.psum_scatter(
        lax.dot_general(
            activations, projected, (((0,), (0,)), ((), ())), preferred_element_type=jnp.float32
        ),
        "dp",
        scatter_dimension=0,
        tiled=True,
    )
    first_next = 0.9 * first_moment + 0.1 * low_grad
    second_next = 0.999 * second_moment + 0.001 * low_grad * low_grad
    first_fix = 1.0 - 0.9**STEP
    second_fix = 1.0 - 0.999**STEP
    normed = (first_next / first_fix / (jnp.sqrt(second_next / second_fix) + 1e-08)).astype(
        jnp.bfloat16
    )
    width = basis.shape[0] // lax.axis_size("dp")
    basis_cols = lax.dynamic_slice_in_dim(basis, lax.axis_index("dp") * width, width, 0)
    product = lax.dot_general(
        lax.all_gather(normed, "dp", axis=0, tiled=True),
        basis_cols,
        (((1,), (1,)), ((), ())),
        preferred_element_type=jnp.float32,
    )
    update = (0.25 * product).astype(jnp.bfloat16)
    return (update, first_next, second_next)


def solution(mesh):
    placed = (
        P(("groups", "dp"), "fsdp"),
        P(("groups", "dp"), "fsdp"),
        P("groups", None),
        P(("groups", "fsdp", "dp"), None),
        P(("groups", "fsdp", "dp"), None),
    )
    return jax.shard_map(
        on_device,
        mesh=mesh,
        in_specs=placed,
        out_specs=(
            P(("groups", "fsdp"), "dp"),
            P(("groups", "fsdp", "dp"), None),
            P(("groups", "fsdp", "dp"), None),
        ),
        check_vma=False,
    )
```

profile of v0, /device:TPU:0, one launch (start us, length us, event | category | flops | bytes accessed | tf_op | source)
XLA Modules:
  0.0 173.6 jit_solution(8115422610651630513)
XLA Ops:
  7.2 0.0 copy-start
  7.2 0.0 reduce-scatter.2.cloned.1.call-start
  7.2 1.8 %copy-done = bf16[768,2048]{1,0:T(8,128)(2,1)S(1)} copy-done((bf16[768,2048]{1,0:T(8,128)(2,1)S(1)}, bf16[768,2048]{1,0:T(8,128)(2,1)}, u32[]{:S(2)}) %copy-start) | copy-done | bytes 3145752
  9.1 2.2 %convolution_bitcast_fusion.1 = f32[768,128]{0,1:T(8,128)S(1)} fusion(bf16[768,2048]{1,0:T(8,128)(2,1)S(1)} %copy-done, bf16[8192,128]{1,0:T(8,128)(2,1)} %param.7, s32[]{:T(128)S(6)} %select_n.6), kind=kOutput, calls=%fused_computation.3 | convolution fusion | flops 402653184 | bytes 4063236 | tf_op jit(solution)/shard_map/dot_general | solution.py:13
  11.3 17.3 %all-reduce.1 = bf16[768,128]{0,1:T(8,128)(2,1)} all-reduce(f32[768,128]{0,1:T(8,128)S(1)} %convolution_bitcast_fusion.1), channel_id=1, replica_groups=mesh['groups'=2,'dp'=4,'fsdp'=4] {'fsdp'}, use_global_device_ids=true, to_apply=%region_0.0 | all-reduce | flops 98304 | bytes 589824 | tf_op jit(solution)/shard_map/psum | solution.py:14
  28.6 7.7 %convolution_bitcast_fusion = f32[7168,128]{0,1:T(8,128)} fusion(bf16[768,7168]{1,0:T(8,128)(2,1)} %param.5, bf16[768,128]{0,1:T(8,128)(2,1)} %all-reduce.1), kind=kOutput, calls=%fused_computation.1 | convolution fusion | flops 1409286144 | bytes 14876672 | tf_op jit(solution)/shard_map/dot_general | solution.py:16
  36.3 0.0 reduce-scatter.2.cloned.1.call-update
  36.3 0.0 all-gather.2.cloned.1.call-start
  36.4 2.4 %copy.8 = f32[1792,128]{0,1:T(8,128)} copy(f32[1792,128]{1,0:T(8,128)} %param.8) | data formatting | bytes 1835008 | tf_op args[3]
  38.8 2.4 %copy.9 = f32[1792,128]{0,1:T(8,128)} copy(f32[1792,128]{1,0:T(8,128)} %param.9) | data formatting | bytes 1835008 | tf_op args[4]
  41.2 64.5 %reduce-scatter.2.cloned.1.call-done = f32[1792,128]{0,1:T(8,128)} async-done(((f32[7168,128]{0,1:T(8,128)}), f32[1792,128]{0,1:T(8,128)}) %reduce-scatter.2.cloned.1.call-update) | async-done | bytes 917520 | tf_op jit(solution)/shard_map/reduce_scatter | solution.py:15
  105.7 3.4 %divide_convert_fusion = (bf16[1792,128]{0,1:T(8,128)(2,1)}, f32[1792,128]{0,1:T(8,128)}, f32[1792,128]{0,1:T(8,128)}) fusion(f32[1792,128]{0,1:T(8,128)} %reduce-scatter.2.cloned.1.call-done, f32[1792,128]{0,1:T(8,128)} %copy.8, f32[1792,128]{0,1:T(8,128)} %copy.9), kind=kLoop, calls=%fused_computation.5 | loop fusion | flops 2752512 | bytes 5046272 | tf_op jit(solution)/shard_map/convert_element_type | solution.py:27
  109.2 0.0 all-gather.2.cloned.1.call-update
  109.2 2.4 %copy.10 = f32[1792,128]{1,0:T(8,128)} copy(f32[1792,128]{0,1:T(8,128)} %get-tuple-element.7) | data formatting | bytes 1835008
  111.6 2.4 %copy.11 = f32[1792,128]{1,0:T(8,128)} copy(f32[1792,128]{0,1:T(8,128)} %get-tuple-element.8) | data formatting | bytes 1835008
  114.0 37.1 %all-gather.2.cloned.1.call-done = bf16[7168,128]{0,1:T(8,128)(2,1)} async-done(((bf16[1792,128]{0,1:T(8,128)(2,1)}), bf16[7168,128]{0,1:T(8,128)(2,1)}) %all-gather.2.cloned.1.call-update) | async-done | bytes 1835024 | tf_op jit(solution)/shard_map/all_gather | solution.py:33
  151.1 15.6 %multiply_convert_fusion = bf16[7168,2048]{1,0:T(8,128)(2,1)} fusion(bf16[7168,128]{0,1:T(8,128)(2,1)} %all-gather.2.cloned.1.call-done, bf16[8192,128]{1,0:T(8,128)(2,1)} %param.7, s32[]{:T(128)S(6)} %select_n.7), kind=kOutput, calls=%fused_computation | convolution fusion | flops 3787456512 | bytes 31719428 | tf_op jit(solution)/shard_map/dot_general | solution.py:32
Async XLA Ops:
  7.2 1.9 %copy-start = (bf16[768,2048]{1,0:T(8,128)(2,1)S(1)}, bf16[768,2048]{1,0:T(8,128)(2,1)}, u32[]{:S(2)}) copy-start(bf16[768,2048]{1,0:T(8,128)(2,1)} %param.6) | copy-start | bytes 9437188
  7.2 98.5 %reduce-scatter.2.cloned.1.call-start = ((), (), s32[]{:S(2)}) async-start(), calls=%async_computation.1 | async-start | bytes 4587520 | tf_op jit(solution)/shard_map/reduce_scatter | solution.py:15
  36.3 114.8 %all-gather.2.cloned.1.call-start = ((), (), s32[]{:S(2)}) async-start(), calls=%async_computation.2 | async-start | bytes 2293760 | tf_op jit(solution)/shard_map/all_gather | solution.py:33
Sparse Core Ops, SparseCore 0:
  36.5 69.2 reduce-scatter.1
  109.3 41.7 all-gather.1
where the time goes:
time: 174 us
  waiting for transfers between devices  102 us (59%)
  matrix products  25.5 us (15%)
  blocking collectives  17.3 us (10%)
  between operations  14.1 us (8%)
  local copies, waits for them, and re-layouts  11.5 us (7%)
  other arithmetic  3.43 us (2%)
    reduce_scatter x1, waiting for transfers between devices, on_device(): lax.psum_scatter(lax.dot_general(activations, projected, (((0,), (0,)), (...  64.5 us
    all_gather x1, waiting for transfers between devices, on_device(): lax.all_gather(normed, 'dp', axis=0, tiled=True)  37.1 us
    psum x1, blocking collectives, on_device(): projected = lax.psum(partial_proj, 'fsdp').astype(jnp.bfloat16)  17.3 us
    dot_general x1, matrix products, on_device(): lax.dot_general(lax.all_gather(normed, 'dp', axis=0, tiled=True), basis_c...  15.6 us
    unnamed x6, local copies, waits for them, and re-layouts  11.5 us
    dot_general x1, matrix products, on_device(): lax.dot_general(activations, projected, (((0,), (0,)), ((), ())), preferr...  7.69 us
  transfers between devices with their start and end apart: 2, of which 2 were waited for; matrix products, arithmetic and copies ran while one was open for 6% of the time, Pallas kernels for 0%

commit v1 on v0

--- a/solution.py
+++ b/solution.py
@@ -1,12 +1,332 @@
+import functools
+
 import jax
 import jax.numpy as jnp
 from jax import lax
+from jax.experimental import pallas as pl
+from jax.experimental.pallas import tpu as pltpu
 from jax.sharding import PartitionSpec as P
 
 STEP = 10
-
-
-def on_device(activations, out_grad, basis, first_moment, second_moment):
+CHUNKS = 2
+VMEM = 16 << 20
+WIDE = 32 << 20
+PIECES = 3
+TOKEN = jax.ShapeDtypeStruct((8, 128), jnp.float32)
+
+
+def cost(flops, moved):
+    return pl.CostEstimate(flops=flops, bytes_accessed=moved, transcendentals=0)
+
+
+def swap(value, axis, bit):
+    n = lax.axis_size(axis)
+    return lax.ppermute(value, axis, [(i, i ^ bit) for i in range(n)])
+
+
+def project(out_grad, basis):
+    tokens, features = out_grad.shape
+    rows, rank = tokens // 2, basis.shape[1]
+
+    def kernel(grad_hbm, basis_hbm, give_ref, keep_ref, grad, base, sems):
+        place = lax.axis_index("fsdp")
+        core = lax.rem(place, 2)
+        copies = [
+            pltpu.make_async_copy(
+                basis_hbm.at[pl.ds(pl.multiple_of(place * features, features), features), :],
+                base,
+                sems.at[0],
+            )
+        ]
+        piece = rows // PIECES
+        for turn, half in enumerate((1 - core, core)):
+            for part in range(PIECES):
+                first = half * rows + part * piece
+                copies.append(
+                    pltpu.make_async_copy(
+                        grad_hbm.at[pl.ds(pl.multiple_of(first, piece), piece), :],
+                        grad.at[turn, pl.ds(part * piece, piece), :],
+                        sems.at[turn * PIECES + part + 1],
+                    )
+                )
+        for copy in copies:
+            copy.start()
+        copies[0].wait()
+        for turn, out_ref in enumerate((give_ref, keep_ref)):
+            for part in range(PIECES):
+                copies[turn * PIECES + part + 1].wait()
+            out_ref[...] = jnp.dot(
+                grad[turn], base[...], preferred_element_type=jnp.float32
+            ).T
+
+    return pl.pallas_call(
+        kernel,
+        in_specs=[pl.BlockSpec(memory_space=pltpu.HBM)] * 2,
+        out_specs=[pl.BlockSpec(memory_space=pltpu.VMEM)] * 2,
+        out_shape=[jax.ShapeDtypeStruct((rank, rows), jnp.float32)] * 2,
+        scratch_shapes=[
+            pltpu.VMEM((2, rows, features), jnp.bfloat16),
+            pltpu.VMEM((features, rank), jnp.bfloat16),
+            pltpu.SemaphoreType.DMA((2 * PIECES + 1,)),
+        ],
+        compiler_params=pltpu.CompilerParams(vmem_limit_bytes=WIDE),
+        cost_estimate=cost(2 * tokens * features * rank, 2 * features * (tokens + rank)),
+        name="project",
+    )(out_grad, basis)
+
+
+def settle(pair, far, after):
+    def kernel(pair_ref, far_ref, after_ref, out_ref):
+        out_ref[...] = (pair_ref[...] + far_ref[...]).astype(jnp.bfloat16)
+
+    return pl.pallas_call(
+        kernel,
+        in_specs=[pl.BlockSpec(memory_space=pltpu.VMEM)] * 2
+        + [pl.BlockSpec(memory_space=pl.ANY)],
+        out_specs=pl.BlockSpec(memory_space=pltpu.VMEM),
+        out_shape=jax.ShapeDtypeStruct(pair.shape, jnp.bfloat16),
+        compiler_params=pltpu.CompilerParams(vmem_limit_bytes=VMEM),
+        cost_estimate=cost(pair.size, 10 * pair.size),
+        name="settle",
+    )(pair, far, after)
+
+
+def blocks_of(act_hbm, held, sems, parts, rows):
+    copies = []
+    for place, (bit, chunk) in enumerate(parts):
+        block = (lax.axis_index("dp") ^ bit) * CHUNKS + chunk
+        copies.append(
+            pltpu.make_async_copy(
+                act_hbm.at[:, pl.ds(pl.multiple_of(block * rows, 128), rows)],
+                held.at[place],
+                sems.at[place],
+            )
+        )
+    for copy in copies:
+        copy.start()
+    return copies
+
+
+def load(activations, parts, after):
+    tokens, units = activations.shape
+    rows = units // (lax.axis_size("dp") * CHUNKS)
+
+    def kernel(act_hbm, after_ref, held, token_ref, sems):
+        for copy in blocks_of(act_hbm, held, sems, parts, rows):
+            copy.wait()
+        token_ref[...] = jnp.zeros_like(token_ref)
+
+    return pl.pallas_call(
+        kernel,
+        in_specs=[pl.BlockSpec(memory_space=pltpu.HBM), pl.BlockSpec(memory_space=pl.ANY)],
+        out_specs=[pl.BlockSpec(memory_space=pltpu.VMEM)] * 2,
+        out_shape=[jax.ShapeDtypeStruct((len(parts), tokens, rows), jnp.bfloat16), TOKEN],
+        scratch_shapes=[pltpu.SemaphoreType.DMA((len(parts),))],
+        compiler_params=pltpu.CompilerParams(vmem_limit_bytes=VMEM),
+        cost_estimate=cost(0, 2 * tokens * rows * len(parts)),
+        name="load",
+    )(activations, after)
+
+
+def term(mine_ref, other_ref, block):
+    first = lax.rem(lax.axis_index("fsdp"), 2) == 0
+    low, high = mine_ref[...], other_ref[...]
+    whole = jnp.concatenate(
+        [jnp.where(first, low, high), jnp.where(first, high, low)], axis=1
+    )
+    return jnp.dot(whole, block, preferred_element_type=jnp.float32).T
+
+
+def low_held(held, mine, other, place, after):
+    rank = mine.shape[0]
+    _, tokens, rows = held.shape
+
+    def kernel(mine_ref, other_ref, act_ref, after_ref, out_ref, token_ref):
+        out_ref[...] = term(mine_ref, other_ref, act_ref[place]).astype(jnp.bfloat16)
+        token_ref[...] = jnp.zeros_like(token_ref)
+
+    return pl.pallas_call(
+        kernel,
+        in_specs=[pl.BlockSpec(memory_space=pltpu.VMEM)] * 3
+        + [pl.BlockSpec(memory_space=pl.ANY)],
+        out_specs=[pl.BlockSpec(memory_space=pltpu.VMEM)] * 2,
+        out_shape=[jax.ShapeDtypeStruct((rows, rank), jnp.bfloat16), TOKEN],
+        compiler_params=pltpu.CompilerParams(vmem_limit_bytes=VMEM),
+        cost_estimate=cost(2 * tokens * rows * rank, 2 * tokens * rows),
+        name="low_held",
+    )(mine, other, held, after)
+
+
+def low_rest(activations, mine, other, parts, kinds, after):
+    rank = mine.shape[0]
+    tokens, units = activations.shape
+    rows = units // (lax.axis_size("dp") * CHUNKS)
+
+    def kernel(mine_ref, other_ref, act_hbm, after_ref, *rest):
+        held, sems = rest[-2:]
+        copies = blocks_of(act_hbm, held, sems, parts, rows)
+        for place, copy in enumerate(copies):
+            copy.wait()
+            rest[place][...] = term(mine_ref, other_ref, held[place]).astype(kinds[place])
+
+    return pl.pallas_call(
+        kernel,
+        grid=(1,),
+        in_specs=[pl.BlockSpec(memory_space=pltpu.VMEM)] * 2
+        + [pl.BlockSpec(memory_space=pltpu.HBM), pl.BlockSpec(memory_space=pl.ANY)],
+        out_specs=[pl.BlockSpec((rows, rank), lambda i: (0, 0))] * len(parts),
+        out_shape=[pltpu.HBM((rows, rank), kind) for kind in kinds],
+        scratch_shapes=[
+            pltpu.VMEM((len(parts), tokens, rows), jnp.bfloat16),
+            pltpu.SemaphoreType.DMA((len(parts),)),
+        ],
+        compiler_params=pltpu.CompilerParams(vmem_limit_bytes=WIDE),
+        cost_estimate=cost(1000, 1000),
+        name="low_rest",
+    )(mine, other, activations, after)
+
+
+def adam(own, near, far, first, second, chunk, before, after=()):
+    rows, rank = own.shape
+    tile = rows // 2
+    first_fix = 1.0 - 0.9**STEP
+    second_fix = 1.0 - 0.999**STEP
+
+    def kernel(own_ref, near_ref, far_ref, first_ref, second_ref, *rest):
+        normed_ref, first_out, second_out = rest[-3:]
+        low = (
+            own_ref[...]
+            + near_ref[...].astype(jnp.float32)
+            + far_ref[...].astype(jnp.float32)
+        )
+        first_next = 0.9 * first_ref[...] + 0.1 * low
+        second_next = 0.999 * second_ref[...] + 0.001 * low * low
+        first_out[...] = first_next
+        second_out[...] = second_next
+        normed_ref[...] = (
+            first_next / first_fix / (jnp.sqrt(second_next / second_fix) + 1e-08)
+        ).astype(jnp.bfloat16)
+
+    local = pl.BlockSpec((tile, rank), lambda i: (i, 0))
+    whole = pl.BlockSpec((tile, rank), lambda i: (chunk * 2 + i, 0))
+    extra = [] if before is None else list(before)
+    return pl.pallas_call(
+        kernel,
+        grid=(2,),
+        in_specs=[local, local, local, whole, whole]
+        + [pl.BlockSpec(memory_space=pl.ANY)] * (len(extra) + len(after)),
+        out_specs=[local, whole, whole],
+        out_shape=[
+            jax.ShapeDtypeStruct((rows, rank), jnp.bfloat16),
+            jax.ShapeDtypeStruct(first.shape, jnp.float32),
+            jax.ShapeDtypeStruct(second.shape, jnp.float32),
+        ],
+        input_output_aliases={5: 1, 6: 2} if extra else {},
+        compiler_params=pltpu.CompilerParams(vmem_limit_bytes=VMEM),
+        cost_estimate=cost(30 * rows * rank, 24 * rows * rank),
+        name="adam",
+    )(own, near, far, first, second, *extra, *after)
+
+
+def expand(place, normed, basis_cols, bit, chunk, shape, before):
+    rows, rank = normed.shape
+    width = basis_cols.shape[0]
+    steps = 2
+    tile = rows // steps
+
+    def kernel(s, normed_ref, basis_ref, *rest):
+        out_ref, token_ref = rest[-2:]
+        product = lax.dot_general(
+            normed_ref[...],
+            basis_ref[...],
+            (((1,), (1,)), ((), ())),
+            preferred_element_type=jnp.float32,
+        )
+        out_ref[...] = (0.25 * product).astype(jnp.bfloat16)
+        token_ref[...] = jnp.zeros_like(token_ref)
+
+    extra = [] if before is None else [before]
+    return pl.pallas_call(
+        kernel,
+        grid_spec=pltpu.PrefetchScalarGridSpec(
+            num_scalar_prefetch=1,
+            grid=(steps,),
+            in_specs=[
+                pl.BlockSpec((tile, rank), lambda i, s: (i, 0)),
+                pl.BlockSpec((width, rank), lambda i, s: (0, 0)),
+            ]
+            + [pl.BlockSpec(memory_space=pl.ANY)] * len(extra),
+            out_specs=[
+                pl.BlockSpec(
+                    (tile, width), lambda i, s: (((s[0] ^ bit) * CHUNKS + chunk) * steps + i, 0)
+                ),
+                pl.BlockSpec((8, 128), lambda i, s: (0, 0)),
+            ],
+        ),
+        out_shape=[
+            jax.ShapeDtypeStruct(shape, jnp.bfloat16),
+            TOKEN,
+        ],
+        input_output_aliases={3: 0} if extra else {},
+        compiler_params=pltpu.CompilerParams(vmem_limit_bytes=VMEM),
+        cost_estimate=cost(60 * rows * rank * width, 60 * rows * width),
+        name="expand",
+    )(place, normed, basis_cols, *extra)
+
+
+def paired(activations, out_grad, basis, first_moment, second_moment):
+    f32, b16 = jnp.float32, jnp.bfloat16
+    z = lax.axis_index("dp")
+    width = basis.shape[0] // lax.axis_size("dp")
+    fixed = functools.partial(pltpu.with_memory_space_constraint, memory_space=pltpu.HBM)
+    shape = (activations.shape[1], width)
+    basis_cols = lax.dynamic_slice_in_dim(basis, z * width, width, 0)
+
+    give, keep = project(fixed(out_grad), fixed(basis))
+    activations = fixed(activations)
+    held, token = load(activations, ((3, 0), (1, 0)), keep)
+    pair = keep + swap(give, "fsdp", 1)
+    mine = settle(pair, swap(pair, "fsdp", 2), token)
+    other = swap(mine, "fsdp", 1)
+
+    cross_a, token = low_held(held, mine, other, 0, token)
+    cross_a = swap(cross_a, "dp", 1)
+    near_a, token = low_held(held, mine, other, 1, token)
+    near_a = swap(near_a, "dp", 1)
+    cross_b, two_a, own_a, two_b, near_b, own_b = low_rest(
+        activations,
+        mine,
+        other,
+        ((3, 1), (2, 0), (0, 0), (2, 1), (1, 1), (0, 1)),
+        (b16, f32, f32, f32, b16, f32),
+        token,
+    )
+    cross_b, near_b = swap(cross_b, "dp", 1), swap(near_b, "dp", 1)
+    sum_a = swap((two_a + cross_a).astype(b16), "dp", 2)
+    sum_b = swap((two_b + cross_b).astype(b16), "dp", 2)
+
+    first_moment, second_moment = fixed(first_moment), fixed(second_moment)
+    grow = functools.partial(expand, z[None])
+    rows_a, *moments = adam(fixed(own_a), near_a, sum_a, first_moment, second_moment, 0, None)
+    far_a = swap(rows_a, "dp", 2)
+    next_a = swap(rows_a, "dp", 1)
+    update, token = grow(rows_a, basis_cols, 0, 0, shape, None)
+    rows_b, *moments = adam(
+        fixed(own_b), near_b, sum_b, first_moment, second_moment, 1, moments, (token,)
+    )
+    far_b = swap(rows_b, "dp", 2)
+    next_b = swap(rows_b, "dp", 1)
+    last_a = swap(far_a, "dp", 1)
+    update, token = grow(next_a, basis_cols, 1, 0, shape, update)
+    update, token = grow(far_a, basis_cols, 2, 0, shape, update)
+    update, token = grow(rows_b, basis_cols, 0, 1, shape, update)
+    last_b = swap(far_b, "dp", 1)
+    for bit, chunk, rows in ((3, 0, last_a), (1, 1, next_b), (2, 1, far_b), (3, 1, last_b)):
+        update, token = grow(rows, basis_cols, bit, chunk, shape, update)
+    return (update, *moments)
+
+
+def general(activations, out_grad, basis, first_moment, second_moment):
     features = out_grad.shape[1]
     fsdp_index = lax.axis_index("fsdp")
     basis_rows = lax.dynamic_slice_in_dim(basis, fsdp_index * features, features, 0)
@@ -47,6 +367,7 @@
         P(("groups", "fsdp", "dp"), None),
         P(("groups", "fsdp", "dp"), None),
     )
+    on_device = paired if mesh.shape["dp"] == 4 and mesh.shape["fsdp"] == 4 else general
     return jax.shard_map(
         on_device,
         mesh=mesh,

time: 174 us -> 90.6 us (0.52)
  waiting for transfers between devices: 102 us -> 33 us
  Pallas kernels: 0 us -> 36.1 us
  matrix products: 25.5 us -> 0 us
  blocking collectives: 17.3 us -> 0 us
  starting transfers between devices: 0.08 us -> 17.2 us
  between operations: 14.1 us -> 0.72 us
  local copies, waits for them, and re-layouts: 11.5 us -> 1.08 us
    reduce_scatter x1 -> x0, waiting for transfers between devices: 64.5 us -> none  [on_device(): lax.psum_scatter(lax.dot_general(activations, projected, (((0,), (0,)), (...]
    all_gather x1 -> x0, waiting for transfers between devices: 37.1 us -> none  [on_device(): lax.all_gather(normed, 'dp', axis=0, tiled=True)]
    pallas_call x0 -> x16, Pallas kernels: none -> 36.1 us  [the longest x8 20.2 us: expand(): pl.pallas_call(kernel, grid_spec=pltpu.PrefetchScalarGridSpec(num_scalar_...]
    ppermute x0 -> x15, waiting for transfers between devices: none -> 33 us  [swap(): return lax.ppermute(value, axis, [(i, i ^ bit) for i in range(n)])]
    dot_general x3 -> x0, matrix products: 25.5 us -> none  [the longest x1 15.6 us: on_device(): lax.dot_general(lax.all_gather(normed, 'dp', axis=0, tiled=True), basis_c...]
    psum x1 -> x0, blocking collectives: 17.3 us -> none  [on_device(): projected = lax.psum(partial_proj, 'fsdp').astype(jnp.bfloat16)]
    ppermute x0 -> x15, starting transfers between devices: none -> 17.2 us  [swap(): return lax.ppermute(value, axis, [(i, i ^ bit) for i in range(n)])]
    unnamed x6 -> x0, local copies, waits for them, and re-layouts: 11.5 us -> none
  transfers between devices with their start and end apart: 2 -> 15, of which waited for: 2 -> 7; matrix products, arithmetic and copies ran while one was open for 6% -> 4% of each run, Pallas kernels for 0% -> 33%
where the time goes in v1:
time: 90.6 us; the launch traced here: 90.2 us
  Pallas kernels  36.1 us (40%)
  waiting for transfers between devices  33 us (36%)
  starting transfers between devices  17.2 us (19%)
  other arithmetic  2.16 us (2%)
  local copies, waits for them, and re-layouts  1.08 us (1%)
    ppermute x15, waiting for transfers between devices, swap(): return lax.ppermute(value, axis, [(i, i ^ bit) for i in range(n)])  33 us
    pallas_call x8, Pallas kernels, expand(): pl.pallas_call(kernel, grid_spec=pltpu.PrefetchScalarGridSpec(num_scalar_...  20.2 us
    ppermute x15, starting transfers between devices, swap(): return lax.ppermute(value, axis, [(i, i ^ bit) for i in range(n)])  17.2 us
    pallas_call x1, Pallas kernels, low_rest(): pl.pallas_call(kernel, grid=(1,), in_specs=[pl.BlockSpec(memory_space=plt...  5.12 us
    pallas_call x2, Pallas kernels, adam(): pl.pallas_call(kernel, grid=(2,), in_specs=[local, local, local, whole, w...  4.51 us
    pallas_call x1, Pallas kernels, project(): pl.pallas_call(kernel, in_specs=[pl.BlockSpec(memory_space=pltpu.HBM)] *...  3.64 us
  transfers between devices with their start and end apart: 15, of which 7 were waited for; matrix products, arithmetic and copies ran while one was open for 4% of the time, Pallas kernels for 33%

profile of v1, /device:TPU:0, one launch (start us, length us, event | category | flops | bytes accessed | tf_op | source)
XLA Modules:
  0.0 90.2 jit_solution(10212640488695025574)
XLA Ops:
  0.6 3.6 %project.1 = (f32[128,384]{1,0:T(8,128)S(1)}, f32[128,384]{1,0:T(8,128)S(1)}) custom-call(bf16[768,2048]{1,0:T(8,128)(2,1)} %grad_hbm.1, bf16[8192,128]{1,0:T(8,128)(2,1)} %basis_hbm.1), custom_call_target="tpu_custom_call" | custom-call | flops 402653184 | bytes 3670016 | tf_op jit(solution)/shard_map/project/pallas_call | solution.py:62
  4.3 0.5 collective-permute-start
  4.8 1.1 %collective-permute-done = f32[128,384]{1,0:T(8,128)S(1)} collective-permute-done((f32[128,384]{1,0:T(8,128)S(1)}, f32[128,384]{1,0:T(8,128)S(1)}, u32[]{:S(2)}, u32[]{:S(2)}) %collective-permute-start) | collective-permute-done | bytes 196640 | tf_op jit(solution)/shard_map/ppermute | solution.py:24
  5.9 2.9 %collective-permute-start.1 = (f32[128,384]{1,0:T(8,128)S(1)}, f32[128,384]{1,0:T(8,128)S(1)}, u32[]{:S(2)}, u32[]{:S(2)}) collective-permute-start(f32[128,384]{1,0:T(8,128)S(1)} %add.12.pair_ref), channel_id=1, source_target_pairs={{0,2},{1,3},{2,0},{3,1},{4,6},{5,7},{6,4},{7,5},{8,10},{9,11},{10,... | collective-permute-start | bytes 589832 | tf_op jit(solution)/shard_map/ppermute | solution.py:24
  8.8 1.8 %load.1 = (bf16[2,768,896]{2,1,0:T(8,128)(2,1)S(1)}, f32[8,128]{1,0:T(8,128)S(1)}) custom-call(bf16[768,7168]{1,0:T(8,128)(2,1)} %act_hbm.3, f32[128,384]{1,0:T(8,128)S(1)} %get-tuple-element.32.after_ref), custom_call_target="tpu_custom_call" | custom-call | bytes 2752512 | tf_op jit(solution)/shard_map/load/pallas_call | solution.py:119
  10.6 3.4 %collective-permute-done.1.far_ref = f32[128,384]{1,0:T(8,128)S(1)} collective-permute-done((f32[128,384]{1,0:T(8,128)S(1)}, f32[128,384]{1,0:T(8,128)S(1)}, u32[]{:S(2)}, u32[]{:S(2)}) %collective-permute-start.1) | collective-permute-done | bytes 196640 | tf_op jit(solution)/shard_map/ppermute | solution.py:24
  14.0 0.1 collective-permute-start.2
  14.1 1.3 %collective-permute-done.2.other_ref = bf16[128,384]{1,0:T(8,128)(2,1)S(1)} collective-permute-done((bf16[128,384]{1,0:T(8,128)(2,1)S(1)}, bf16[128,384]{1,0:T(8,128)(2,1)S(1)}, u32[]{:S(2)}, u32[]{:S(2)}) %collective-permute-start.2) | collective-permute-done | bytes 98336 | tf_op jit(solution)/shard_map/ppermute | solution.py:24
  15.4 0.4 low_held.2
  15.9 1.9 %collective-permute-start.7 = (bf16[896,128]{1,0:T(8,128)(2,1)S(1)}, bf16[896,128]{1,0:T(8,128)(2,1)S(1)}, u32[]{:S(2)}, u32[]{:S(2)}) collective-permute-start(bf16[896,128]{1,0:T(8,128)(2,1)S(1)} %get-tuple-element.45), channel_id=1, source_target_pairs={{0,4},{4,0},{8,12},{12,8},{1,5},{5,1},{9,13},{13,9},{2,6},{6,2},{1... | collective-permute-start | bytes 688136 | tf_op jit(solution)/shard_map/ppermute | solution.py:24
  17.8 1.1 %constant_dynamic-slice_fusion.basis_ref = bf16[2048,128]{1,0:T(8,128)(2,1)S(1)} fusion(bf16[8192,128]{1,0:T(8,128)(2,1)} %basis_hbm.1, s32[]{:T(128)S(6)} %select_n.3), kind=kLoop, calls=%fused_computation.2 | loop fusion | bytes 1048580 | tf_op jit(solution)/shard_map/dynamic_slice | solution.py:283
  18.8 0.4 low_held.3
  19.3 0.3 collective-permute-start.6
  19.6 5.1 %low_rest.1 = (bf16[896,128]{1,0:T(8,128)(2,1)}, f32[896,128]{1,0:T(8,128)}, f32[896,128]{1,0:T(8,128)}, f32[896,128]{1,0:T(8,128)}, bf16[896,128]{1,0:T(8,128)(2,1)}, /*index=5*/f32[896,128]{1,0:T(8,128)}) custom-call(bf16[128,384]{1,0:T(8,128)(2,1)S(1)} %settle.1.mine_ref, bf16[128,384]{1,0:T(8,128)(2,1)S(1)} %collective-permute-done.2.other_ref, ...), custom_call_target="tpu_custom_call" | custom-call | flops 1000 | bytes 1000 | tf_op jit(solution)/shard_map/low_rest/pallas_call | solution.py:172
  24.7 1.9 %collective-permute-start.3 = (bf16[896,128]{1,0:T(8,128)(2,1)}, bf16[896,128]{1,0:T(8,128)(2,1)S(1)}, u32[]{:S(2)}, u32[]{:S(2)}) collective-permute-start(bf16[896,128]{1,0:T(8,128)(2,1)} %get-tuple-element.39), channel_id=1, source_target_pairs={{0,4},{4,0},{8,12},{12,8},{1,5},{5,1},{9,13},{13,9},{2,6},{6,2},{1... | collective-permute-start | bytes 688136 | tf_op jit(solution)/shard_map/ppermute | solution.py:24
  26.6 0.2 collective-permute-start.4
  26.8 0.0 collective-permute-done.7
  26.8 1.1 %add_convert_fusion = bf16[896,128]{1,0:T(8,128)(2,1)S(1)} fusion(f32[896,128]{1,0:T(8,128)} %get-tuple-element.44, bf16[896,128]{1,0:T(8,128)(2,1)S(1)} %collective-permute-done.7), kind=kLoop, calls=%fused_computation | loop fusion | flops 344064 | bytes 917504 | tf_op jit(solution)/shard_map/convert_element_type | solution.py:305
  27.9 2.9 %collective-permute-start.8 = (bf16[896,128]{1,0:T(8,128)(2,1)S(1)}, bf16[896,128]{1,0:T(8,128)(2,1)S(1)}, u32[]{:S(2)}, u32[]{:S(2)}) collective-permute-start(bf16[896,128]{1,0:T(8,128)(2,1)S(1)} %add_convert_fusion), channel_id=1, source_target_pairs={{0,8},{4,12},{8,0},{12,4},{1,9},{5,13},{9,1},{13,5},{2,10},{6,14},... | collective-permute-start | bytes 688136 | tf_op jit(solution)/shard_map/ppermute | solution.py:24
  30.8 12.6 %collective-permute-done.4 = bf16[896,128]{1,0:T(8,128)(2,1)S(1)} collective-permute-done((bf16[896,128]{1,0:T(8,128)(2,1)}, bf16[896,128]{1,0:T(8,128)(2,1)S(1)}, u32[]{:S(2)}, u32[]{:S(2)}) %collective-permute-start.4) | collective-permute-done | bytes 229408 | tf_op jit(solution)/shard_map/ppermute | solution.py:24
  43.3 1.1 %add_convert_fusion.1 = bf16[896,128]{1,0:T(8,128)(2,1)S(1)} fusion(f32[896,128]{1,0:T(8,128)} %get-tuple-element.40, bf16[896,128]{1,0:T(8,128)(2,1)S(1)} %collective-permute-done.4), kind=kLoop, calls=%fused_computation.1 | loop fusion | flops 344064 | bytes 917504 | tf_op jit(solution)/shard_map/convert_element_type | solution.py:306
  44.4 2.0 %collective-permute-start.5 = (bf16[896,128]{1,0:T(8,128)(2,1)S(1)}, bf16[896,128]{1,0:T(8,128)(2,1)S(1)}, u32[]{:S(2)}, u32[]{:S(2)}) collective-permute-start(bf16[896,128]{1,0:T(8,128)(2,1)S(1)} %add_convert_fusion.1), channel_id=1, source_target_pairs={{0,8},{4,12},{8,0},{12,4},{1,9},{5,13},{9,1},{13,5},{2,10},{6,14},... | collective-permute-start | bytes 688136 | tf_op jit(solution)/shard_map/ppermute | solution.py:24
  46.4 0.0 collective-permute-done.6.near_ref
  46.4 0.0 collective-permute-done.8.far_ref
  46.4 2.3 %adam.2 = (bf16[896,128]{1,0:T(8,128)(2,1)S(1)}, f32[1792,128]{1,0:T(8,128)}, f32[1792,128]{1,0:T(8,128)}) custom-call(f32[896,128]{1,0:T(8,128)} %get-tuple-element.42.own_ref, bf16[896,128]{1,0:T(8,128)(2,1)S(1)} %collective-permute-done.6.near_ref, bf16[896,128]{1,0:T(8,128)(2,1)S(1)} %collective-permute-done.8.far_ref, f32[1792,128]{1,0:T(8,128)} %first_ref.3, ...), custom_call_target="tpu_custom_call" | custom-call | flops 3440640 | bytes 2752512 | tf_op jit(solution)/shard_map/adam/pallas_call | solution.py:213
  48.7 2.4 %collective-permute-start.14 = (bf16[896,128]{1,0:T(8,128)(2,1)S(1)}, bf16[896,128]{1,0:T(8,128)(2,1)S(1)}, u32[]{:S(2)}, u32[]{:S(2)}) collective-permute-start(bf16[896,128]{1,0:T(8,128)(2,1)S(1)} %get-tuple-element.48.normed_ref), channel_id=1, source_target_pairs={{0,4},{4,0},{8,12},{12,8},{1,5},{5,1},{9,13},{13,9},{2,6},{6,2},{1... | collective-permute-start | bytes 688136 | tf_op jit(solution)/shard_map/ppermute | solution.py:24
  51.1 0.0 collective-permute-start.12
  51.1 2.5 %expand.8 = (bf16[7168,2048]{1,0:T(8,128)(2,1)}, f32[8,128]{1,0:T(8,128)S(1)}) custom-call(s32[1]{0:T(128)} %bitcast.s, bf16[896,128]{1,0:T(8,128)(2,1)S(1)} %get-tuple-element.48.normed_ref, bf16[2048,128]{1,0:T(8,128)(2,1)S(1)} %constant_dynamic-slice_fusion.basis_ref), custom_call_target="tpu_custom_call" | custom-call | flops 14092861440 | bytes 110100480 | tf_op jit(solution)/shard_map/expand/pallas_call | solution.py:249
  53.6 0.0 collective-permute-done.3.near_ref
  53.6 9.8 %collective-permute-done.5.far_ref = bf16[896,128]{1,0:T(8,128)(2,1)S(1)} collective-permute-done((bf16[896,128]{1,0:T(8,128)(2,1)S(1)}, bf16[896,128]{1,0:T(8,128)(2,1)S(1)}, u32[]{:S(2)}, u32[]{:S(2)}) %collective-permute-start.5) | collective-permute-done | bytes 229408 | tf_op jit(solution)/shard_map/ppermute | solution.py:24
  63.5 2.2 %adam.3 = (bf16[896,128]{1,0:T(8,128)(2,1)S(1)}, f32[1792,128]{1,0:T(8,128)}, f32[1792,128]{1,0:T(8,128)}) custom-call(f32[896,128]{1,0:T(8,128)} %get-tuple-element.38.own_ref, bf16[896,128]{1,0:T(8,128)(2,1)S(1)} %collective-permute-done.3.near_ref, ...), custom_call_target="tpu_custom_call", output_to_operand_aliasing={{1}: (5, {}), {2}: (6, {})} | custom-call | flops 3440640 | bytes 2752512 | tf_op jit(solution)/shard_map/adam/pallas_call | solution.py:213
  65.7 0.0 collective-permute-start.11
  65.7 0.0 collective-permute-start.9
  65.8 2.6 %collective-permute-done.12.normed_ref = bf16[896,128]{1,0:T(8,128)(2,1)S(1)} collective-permute-done((bf16[896,128]{1,0:T(8,128)(2,1)S(1)}, bf16[896,128]{1,0:T(8,128)(2,1)S(1)}, u32[]{:S(2)}, u32[]{:S(2)}) %collective-permute-start.12) | collective-permute-done | bytes 229408 | tf_op jit(solution)/shard_map/ppermute | solution.py:24
  68.4 1.3 %collective-permute-start.13 = (bf16[896,128]{1,0:T(8,128)(2,1)S(1)}, bf16[896,128]{1,0:T(8,128)(2,1)S(1)}, u32[]{:S(2)}, u32[]{:S(2)}) collective-permute-start(bf16[896,128]{1,0:T(8,128)(2,1)S(1)} %collective-permute-done.12.normed_ref), channel_id=1, source_target_pairs={{0,4},{4,0},{8,12},{12,8},{1,5},{5,1},{9,13},{13,9},{2,6},{6,2},{1... | collective-permute-start | bytes 688136 | tf_op jit(solution)/shard_map/ppermute | solution.py:24
  69.7 0.0 collective-permute-done.14.normed_ref
  69.7 2.5 %expand.9 = (bf16[7168,2048]{1,0:T(8,128)(2,1)}, f32[8,128]{1,0:T(8,128)}) custom-call(s32[1]{0:T(128)} %bitcast.s, bf16[896,128]{1,0:T(8,128)(2,1)S(1)} %collective-permute-done.14.normed_ref, bf16[2048,128]{1,0:T(8,128)(2,1)S(1)} %constant_dynamic-slice_fusion.basis_ref, bf16[7168,2048]{1,0:T(8,128)(2,1)} %get-tuple-element.51.rest_0_), custom_call_target="tpu_custom_call", output_to_operand_aliasing={{0}: (3, {})} | custom-call | flops 14092861440 | bytes 110100480 | tf_op jit(solution)/shard_map/expand/pallas_call | solution.py:249
  72.2 2.5 %expand.10 = (bf16[7168,2048]{1,0:T(8,128)(2,1)}, f32[8,128]{1,0:T(8,128)}) custom-call(s32[1]{0:T(128)} %bitcast.s, bf16[896,128]{1,0:T(8,128)(2,1)S(1)} %collective-permute-done.12.normed_ref, bf16[2048,128]{1,0:T(8,128)(2,1)S(1)} %constant_dynamic-slice_fusion.basis_ref, bf16[7168,2048]{1,0:T(8,128)(2,1)} %get-tuple-element.52.rest_0_), custom_call_target="tpu_custom_call", output_to_operand_aliasing={{0}: (3, {})} | custom-call | flops 14092861440 | bytes 110100480 | tf_op jit(solution)/shard_map/expand/pallas_call | solution.py:249
  74.7 2.5 %expand.11 = (bf16[7168,2048]{1,0:T(8,128)(2,1)}, f32[8,128]{1,0:T(8,128)}) custom-call(s32[1]{0:T(128)} %bitcast.s, bf16[896,128]{1,0:T(8,128)(2,1)S(1)} %get-tuple-element.50.normed_ref, bf16[2048,128]{1,0:T(8,128)(2,1)S(1)} %constant_dynamic-slice_fusion.basis_ref, bf16[7168,2048]{1,0:T(8,128)(2,1)} %get-tuple-element.53.rest_0_), custom_call_target="tpu_custom_call", output_to_operand_aliasing={{0}: (3, {})} | custom-call | flops 14092861440 | bytes 110100480 | tf_op jit(solution)/shard_map/expand/pallas_call | solution.py:249
  77.2 0.0 collective-permute-done.9.normed_ref
  77.2 0.7 collective-permute-start.10
  78.0 2.1 %collective-permute-done.13.normed_ref = bf16[896,128]{1,0:T(8,128)(2,1)S(1)} collective-permute-done((bf16[896,128]{1,0:T(8,128)(2,1)S(1)}, bf16[896,128]{1,0:T(8,128)(2,1)S(1)}, u32[]{:S(2)}, u32[]{:S(2)}) %collective-permute-start.13) | collective-permute-done | bytes 229408 | tf_op jit(solution)/shard_map/ppermute | solution.py:24
  80.1 2.5 %expand.12 = (bf16[7168,2048]{1,0:T(8,128)(2,1)}, f32[8,128]{1,0:T(8,128)}) custom-call(s32[1]{0:T(128)} %bitcast.s, bf16[896,128]{1,0:T(8,128)(2,1)S(1)} %collective-permute-done.13.normed_ref, bf16[2048,128]{1,0:T(8,128)(2,1)S(1)} %constant_dynamic-slice_fusion.basis_ref, bf16[7168,2048]{1,0:T(8,128)(2,1)} %get-tuple-element.54.rest_0_), custom_call_target="tpu_custom_call", output_to_operand_aliasing={{0}: (3, {})} | custom-call | flops 14092861440 | bytes 110100480 | tf_op jit(solution)/shard_map/expand/pallas_call | solution.py:249
  82.6 0.0 collective-permute-done.11.normed_ref
  82.6 2.5 %expand.13 = (bf16[7168,2048]{1,0:T(8,128)(2,1)}, f32[8,128]{1,0:T(8,128)}) custom-call(s32[1]{0:T(128)} %bitcast.s, bf16[896,128]{1,0:T(8,128)(2,1)S(1)} %collective-permute-done.11.normed_ref, bf16[2048,128]{1,0:T(8,128)(2,1)S(1)} %constant_dynamic-slice_fusion.basis_ref, bf16[7168,2048]{1,0:T(8,128)(2,1)} %get-tuple-element.55.rest_0_), custom_call_target="tpu_custom_call", output_to_operand_aliasing={{0}: (3, {})} | custom-call | flops 14092861440 | bytes 110100480 | tf_op jit(solution)/shard_map/expand/pallas_call | solution.py:249
  85.2 2.5 %expand.14 = (bf16[7168,2048]{1,0:T(8,128)(2,1)}, f32[8,128]{1,0:T(8,128)}) custom-call(s32[1]{0:T(128)} %bitcast.s, bf16[896,128]{1,0:T(8,128)(2,1)S(1)} %collective-permute-done.9.normed_ref, bf16[2048,128]{1,0:T(8,128)(2,1)S(1)} %constant_dynamic-slice_fusion.basis_ref, bf16[7168,2048]{1,0:T(8,128)(2,1)} %get-tuple-element.56.rest_0_), custom_call_target="tpu_custom_call", output_to_operand_aliasing={{0}: (3, {})} | custom-call | flops 14092861440 | bytes 110100480 | tf_op jit(solution)/shard_map/expand/pallas_call | solution.py:249
  87.7 0.0 collective-permute-done.10.normed_ref
  87.7 2.5 %expand.15 = (bf16[7168,2048]{1,0:T(8,128)(2,1)}, f32[8,128]{1,0:T(8,128)}) custom-call(s32[1]{0:T(128)} %bitcast.s, bf16[896,128]{1,0:T(8,128)(2,1)S(1)} %collective-permute-done.10.normed_ref, bf16[2048,128]{1,0:T(8,128)(2,1)S(1)} %constant_dynamic-slice_fusion.basis_ref, bf16[7168,2048]{1,0:T(8,128)(2,1)} %get-tuple-element.57.rest_0_), custom_call_target="tpu_custom_call", output_to_operand_aliasing={{0}: (3, {})} | custom-call | flops 14092861440 | bytes 110100480 | tf_op jit(solution)/shard_map/expand/pallas_call | solution.py:249
  (2 shorter events, 0.0 us)
Async XLA Ops:
  4.3 1.6 %collective-permute-start = (f32[128,384]{1,0:T(8,128)S(1)}, f32[128,384]{1,0:T(8,128)S(1)}, u32[]{:S(2)}, u32[]{:S(2)}) collective-permute-start(f32[128,384]{1,0:T(8,128)S(1)} %get-tuple-element.33), channel_id=1, source_target_pairs={{0,1},{1,0},{2,3},{3,2},{4,5},{5,4},{6,7},{7,6},{8,9},{9,8},{10,11... | collective-permute-start | bytes 589832 | tf_op jit(solution)/shard_map/ppermute | solution.py:24
  5.9 8.1 %collective-permute-start.1 = (f32[128,384]{1,0:T(8,128)S(1)}, f32[128,384]{1,0:T(8,128)S(1)}, u32[]{:S(2)}, u32[]{:S(2)}) collective-permute-start(f32[128,384]{1,0:T(8,128)S(1)} %add.12.pair_ref), channel_id=1, source_target_pairs={{0,2},{1,3},{2,0},{3,1},{4,6},{5,7},{6,4},{7,5},{8,10},{9,11},{10,... | collective-permute-start | bytes 589832 | tf_op jit(solution)/shard_map/ppermute | solution.py:24
  14.0 1.4 %collective-permute-start.2 = (bf16[128,384]{1,0:T(8,128)(2,1)S(1)}, bf16[128,384]{1,0:T(8,128)(2,1)S(1)}, u32[]{:S(2)}, u32[]{:S(2)}) collective-permute-start(bf16[128,384]{1,0:T(8,128)(2,1)S(1)} %settle.1.mine_ref), channel_id=1, source_target_pairs={{0,1},{1,0},{2,3},{3,2},{4,5},{5,4},{6,7},{7,6},{8,9},{9,8},{10,11... | collective-permute-start | bytes 294920 | tf_op jit(solution)/shard_map/ppermute | solution.py:24
  15.9 10.9 %collective-permute-start.7 = (bf16[896,128]{1,0:T(8,128)(2,1)S(1)}, bf16[896,128]{1,0:T(8,128)(2,1)S(1)}, u32[]{:S(2)}, u32[]{:S(2)}) collective-permute-start(bf16[896,128]{1,0:T(8,128)(2,1)S(1)} %get-tuple-element.45), channel_id=1, source_target_pairs={{0,4},{4,0},{8,12},{12,8},{1,5},{5,1},{9,13},{13,9},{2,6},{6,2},{1... | collective-permute-start | bytes 688136 | tf_op jit(solution)/shard_map/ppermute | solution.py:24
  19.3 27.1 %collective-permute-start.6 = (bf16[896,128]{1,0:T(8,128)(2,1)S(1)}, bf16[896,128]{1,0:T(8,128)(2,1)S(1)}, u32[]{:S(2)}, u32[]{:S(2)}) collective-permute-start(bf16[896,128]{1,0:T(8,128)(2,1)S(1)} %get-tuple-element.43), channel_id=1, source_target_pairs={{0,4},{4,0},{8,12},{12,8},{1,5},{5,1},{9,13},{13,9},{2,6},{6,2},{1... | collective-permute-start | bytes 688136 | tf_op jit(solution)/shard_map/ppermute | solution.py:24
  24.7 29.0 %collective-permute-start.3 = (bf16[896,128]{1,0:T(8,128)(2,1)}, bf16[896,128]{1,0:T(8,128)(2,1)S(1)}, u32[]{:S(2)}, u32[]{:S(2)}) collective-permute-start(bf16[896,128]{1,0:T(8,128)(2,1)} %get-tuple-element.39), channel_id=1, source_target_pairs={{0,4},{4,0},{8,12},{12,8},{1,5},{5,1},{9,13},{13,9},{2,6},{6,2},{1... | collective-permute-start | bytes 688136 | tf_op jit(solution)/shard_map/ppermute | solution.py:24
  26.6 16.8 %collective-permute-start.4 = (bf16[896,128]{1,0:T(8,128)(2,1)}, bf16[896,128]{1,0:T(8,128)(2,1)S(1)}, u32[]{:S(2)}, u32[]{:S(2)}) collective-permute-start(bf16[896,128]{1,0:T(8,128)(2,1)} %get-tuple-element.41), channel_id=1, source_target_pairs={{0,4},{4,0},{8,12},{12,8},{1,5},{5,1},{9,13},{13,9},{2,6},{6,2},{1... | collective-permute-start | bytes 688136 | tf_op jit(solution)/shard_map/ppermute | solution.py:24
  27.9 18.6 %collective-permute-start.8 = (bf16[896,128]{1,0:T(8,128)(2,1)S(1)}, bf16[896,128]{1,0:T(8,128)(2,1)S(1)}, u32[]{:S(2)}, u32[]{:S(2)}) collective-permute-start(bf16[896,128]{1,0:T(8,128)(2,1)S(1)} %add_convert_fusion), channel_id=1, source_target_pairs={{0,8},{4,12},{8,0},{12,4},{1,9},{5,13},{9,1},{13,5},{2,10},{6,14},... | collective-permute-start | bytes 688136 | tf_op jit(solution)/shard_map/ppermute | solution.py:24
  44.4 19.1 %collective-permute-start.5 = (bf16[896,128]{1,0:T(8,128)(2,1)S(1)}, bf16[896,128]{1,0:T(8,128)(2,1)S(1)}, u32[]{:S(2)}, u32[]{:S(2)}) collective-permute-start(bf16[896,128]{1,0:T(8,128)(2,1)S(1)} %add_convert_fusion.1), channel_id=1, source_target_pairs={{0,8},{4,12},{8,0},{12,4},{1,9},{5,13},{9,1},{13,5},{2,10},{6,14},... | collective-permute-start | bytes 688136 | tf_op jit(solution)/shard_map/ppermute | solution.py:24
  48.7 21.0 %collective-permute-start.14 = (bf16[896,128]{1,0:T(8,128)(2,1)S(1)}, bf16[896,128]{1,0:T(8,128)(2,1)S(1)}, u32[]{:S(2)}, u32[]{:S(2)}) collective-permute-start(bf16[896,128]{1,0:T(8,128)(2,1)S(1)} %get-tuple-element.48.normed_ref), channel_id=1, source_target_pairs={{0,4},{4,0},{8,12},{12,8},{1,5},{5,1},{9,13},{13,9},{2,6},{6,2},{1... | collective-permute-start | bytes 688136 | tf_op jit(solution)/shard_map/ppermute | solution.py:24
  51.1 17.3 %collective-permute-start.12 = (bf16[896,128]{1,0:T(8,128)(2,1)S(1)}, bf16[896,128]{1,0:T(8,128)(2,1)S(1)}, u32[]{:S(2)}, u32[]{:S(2)}) collective-permute-start(bf16[896,128]{1,0:T(8,128)(2,1)S(1)} %get-tuple-element.48.normed_ref), channel_id=1, source_target_pairs={{0,8},{4,12},{8,0},{12,4},{1,9},{5,13},{9,1},{13,5},{2,10},{6,14},... | collective-permute-start | bytes 688136 | tf_op jit(solution)/shard_map/ppermute | solution.py:24
  65.7 16.9 %collective-permute-start.11 = (bf16[896,128]{1,0:T(8,128)(2,1)S(1)}, bf16[896,128]{1,0:T(8,128)(2,1)S(1)}, u32[]{:S(2)}, u32[]{:S(2)}) collective-permute-start(bf16[896,128]{1,0:T(8,128)(2,1)S(1)} %get-tuple-element.50.normed_ref), channel_id=1, source_target_pairs={{0,4},{4,0},{8,12},{12,8},{1,5},{5,1},{9,13},{13,9},{2,6},{6,2},{1... | collective-permute-start | bytes 688136 | tf_op jit(solution)/shard_map/ppermute | solution.py:24
  65.7 11.5 %collective-permute-start.9 = (bf16[896,128]{1,0:T(8,128)(2,1)S(1)}, bf16[896,128]{1,0:T(8,128)(2,1)S(1)}, u32[]{:S(2)}, u32[]{:S(2)}) collective-permute-start(bf16[896,128]{1,0:T(8,128)(2,1)S(1)} %get-tuple-element.50.normed_ref), channel_id=1, source_target_pairs={{0,8},{4,12},{8,0},{12,4},{1,9},{5,13},{9,1},{13,5},{2,10},{6,14},... | collective-permute-start | bytes 688136 | tf_op jit(solution)/shard_map/ppermute | solution.py:24
  68.4 11.7 %collective-permute-start.13 = (bf16[896,128]{1,0:T(8,128)(2,1)S(1)}, bf16[896,128]{1,0:T(8,128)(2,1)S(1)}, u32[]{:S(2)}, u32[]{:S(2)}) collective-permute-start(bf16[896,128]{1,0:T(8,128)(2,1)S(1)} %collective-permute-done.12.normed_ref), channel_id=1, source_target_pairs={{0,4},{4,0},{8,12},{12,8},{1,5},{5,1},{9,13},{13,9},{2,6},{6,2},{1... | collective-permute-start | bytes 688136 | tf_op jit(solution)/shard_map/ppermute | solution.py:24
  77.2 10.4 %collective-permute-start.10 = (bf16[896,128]{1,0:T(8,128)(2,1)S(1)}, bf16[896,128]{1,0:T(8,128)(2,1)S(1)}, u32[]{:S(2)}, u32[]{:S(2)}) collective-permute-start(bf16[896,128]{1,0:T(8,128)(2,1)S(1)} %collective-permute-done.9.normed_ref), channel_id=1, source_target_pairs={{0,4},{4,0},{8,12},{12,8},{1,5},{5,1},{9,13},{13,9},{2,6},{6,2},{1... | collective-permute-start | bytes 688136 | tf_op jit(solution)/shard_map/ppermute | solution.py:24

commit v2 on v1

--- a/solution.py
+++ b/solution.py
@@ -24,13 +24,15 @@
     return lax.ppermute(value, axis, [(i, i ^ bit) for i in range(n)])
 
 
-def project(out_grad, basis):
+def project(out_grad, basis, turn, after=()):
     tokens, features = out_grad.shape
     rows, rank = tokens // 2, basis.shape[1]
-
-    def kernel(grad_hbm, basis_hbm, give_ref, keep_ref, grad, base, sems):
+    piece = rows // PIECES
+
+    def kernel(grad_hbm, basis_hbm, *rest):
+        out_ref, grad, base, sems = rest[-4:]
         place = lax.axis_index("fsdp")
-        core = lax.rem(place, 2)
+        half = lax.rem(place + 1 + turn, 2)
         copies = [
             pltpu.make_async_copy(
                 basis_hbm.at[pl.ds(pl.multiple_of(place * features, features), features), :],
@@ -38,41 +40,38 @@
                 sems.at[0],
             )
         ]
-        piece = rows // PIECES
-        for turn, half in enumerate((1 - core, core)):
-            for part in range(PIECES):
-                first = half * rows + part * piece
-                copies.append(
-                    pltpu.make_async_copy(
-                        grad_hbm.at[pl.ds(pl.multiple_of(first, piece), piece), :],
-                        grad.at[turn, pl.ds(part * piece, piece), :],
-                        sems.at[turn * PIECES + part + 1],
-                    )
+        for part in range(PIECES):
+            first = half * rows + part * piece
+            copies.append(
+                pltpu.make_async_copy(
+                    grad_hbm.at[pl.ds(pl.multiple_of(first, piece), piece), :],
+                    grad.at[pl.ds(part * piece, piece), :],
+                    sems.at[part + 1],
                 )
+            )
         for copy in copies:
             copy.start()
-        copies[0].wait()
-        for turn, out_ref in enumerate((give_ref, keep_ref)):
-            for part in range(PIECES):
-                copies[turn * PIECES + part + 1].wait()
-            out_ref[...] = jnp.dot(
-                grad[turn], base[...], preferred_element_type=jnp.float32
-            ).T
-
-    return pl.pallas_call(
-        kernel,
-        in_specs=[pl.BlockSpec(memory_space=pltpu.HBM)] * 2,
-        out_specs=[pl.BlockSpec(memory_space=pltpu.VMEM)] * 2,
-        out_shape=[jax.ShapeDtypeStruct((rank, rows), jnp.float32)] * 2,
+        for copy in copies:
+            copy.wait()
+        out_ref[...] = jnp.dot(
+            grad[...], base[...], preferred_element_type=jnp.float32
+        ).T
+
+    return pl.pallas_call(
+        kernel,
+        in_specs=[pl.BlockSpec(memory_space=pltpu.HBM)] * 2
+        + [pl.BlockSpec(memory_space=pl.ANY)] * len(after),
+        out_specs=pl.BlockSpec(memory_space=pltpu.VMEM),
+        out_shape=jax.ShapeDtypeStruct((rank, rows), jnp.float32),
         scratch_shapes=[
-            pltpu.VMEM((2, rows, features), jnp.bfloat16),
+            pltpu.VMEM((rows, features), jnp.bfloat16),
             pltpu.VMEM((features, rank), jnp.bfloat16),
-            pltpu.SemaphoreType.DMA((2 * PIECES + 1,)),
+            pltpu.SemaphoreType.DMA((PIECES + 1,)),
         ],
-        compiler_params=pltpu.CompilerParams(vmem_limit_bytes=WIDE),
-        cost_estimate=cost(2 * tokens * features * rank, 2 * features * (tokens + rank)),
+        compiler_params=pltpu.CompilerParams(vmem_limit_bytes=VMEM),
+        cost_estimate=cost(1000, 1000),
         name="project",
-    )(out_grad, basis)
+    )(out_grad, basis, *after)
 
 
 def settle(pair, far, after):
@@ -89,6 +88,40 @@
         cost_estimate=cost(pair.size, 10 * pair.size),
         name="settle",
     )(pair, far, after)
+
+
+def merge(own, got, waiting):
+    def kernel(own_ref, got_ref, waiting_ref, out_ref, next_ref):
+        out_ref[...] = (own_ref[...] + got_ref[...].astype(jnp.float32)).astype(jnp.bfloat16)
+        next_ref[...] = waiting_ref[...]
+
+    return pl.pallas_call(
+        kernel,
+        in_specs=[pl.BlockSpec(memory_space=pltpu.VMEM)] * 3,
+        out_specs=[pl.BlockSpec(memory_space=pltpu.VMEM)] * 2,
+        out_shape=[
+            jax.ShapeDtypeStruct(got.shape, jnp.bfloat16),
+            jax.ShapeDtypeStruct(waiting.shape, jnp.bfloat16),
+        ],
+        compiler_params=pltpu.CompilerParams(vmem_limit_bytes=VMEM),
+        cost_estimate=cost(own.size, 8 * own.size),
+        name="merge",
+    )(own, got, waiting)
+
+
+def pass_on(value, after):
+    def kernel(value_ref, after_ref, out_ref):
+        out_ref[...] = value_ref[...]
+
+    return pl.pallas_call(
+        kernel,
+        in_specs=[pl.BlockSpec(memory_space=pltpu.VMEM), pl.BlockSpec(memory_space=pl.ANY)],
+        out_specs=pl.BlockSpec(memory_space=pltpu.VMEM),
+        out_shape=jax.ShapeDtypeStruct(value.shape, value.dtype),
+        compiler_params=pltpu.CompilerParams(vmem_limit_bytes=VMEM),
+        cost_estimate=cost(0, 4 * value.size),
+        name="pass_on",
+    )(value, after)
 
 
 def blocks_of(act_hbm, held, sems, parts, rows):
@@ -107,25 +140,36 @@
     return copies
 
 
-def load(activations, parts, after):
+def load(activations, basis, parts, after):
     tokens, units = activations.shape
     rows = units // (lax.axis_size("dp") * CHUNKS)
-
-    def kernel(act_hbm, after_ref, held, token_ref, sems):
+    width, rank = basis.shape[0] // lax.axis_size("dp"), basis.shape[1]
+
+    def kernel(act_hbm, basis_hbm, after_ref, held, columns, token_ref, sems):
+        first = pl.multiple_of(lax.axis_index("dp") * width, width)
+        extra = pltpu.make_async_copy(
+            basis_hbm.at[pl.ds(first, width), :], columns, sems.at[len(parts)]
+        )
+        extra.start()
         for copy in blocks_of(act_hbm, held, sems, parts, rows):
             copy.wait()
+        extra.wait()
         token_ref[...] = jnp.zeros_like(token_ref)
 
     return pl.pallas_call(
         kernel,
-        in_specs=[pl.BlockSpec(memory_space=pltpu.HBM), pl.BlockSpec(memory_space=pl.ANY)],
-        out_specs=[pl.BlockSpec(memory_space=pltpu.VMEM)] * 2,
-        out_shape=[jax.ShapeDtypeStruct((len(parts), tokens, rows), jnp.bfloat16), TOKEN],
-        scratch_shapes=[pltpu.SemaphoreType.DMA((len(parts),))],
+        in_specs=[pl.BlockSpec(memory_space=pltpu.HBM)] * 2 + [pl.BlockSpec(memory_space=pl.ANY)],
+        out_specs=[pl.BlockSpec(memory_space=pltpu.VMEM)] * 3,
+        out_shape=[
+            jax.ShapeDtypeStruct((len(parts), tokens, rows), jnp.bfloat16),
+            jax.ShapeDtypeStruct((width, rank), jnp.bfloat16),
+            TOKEN,
+        ],
+        scratch_shapes=[pltpu.SemaphoreType.DMA((len(parts) + 1,))],
         compiler_params=pltpu.CompilerParams(vmem_limit_bytes=VMEM),
         cost_estimate=cost(0, 2 * tokens * rows * len(parts)),
         name="load",
-    )(activations, after)
+    )(activations, basis, after)
 
 
 def term(mine_ref, other_ref, block):
@@ -157,25 +201,32 @@
     )(mine, other, held, after)
 
 
-def low_rest(activations, mine, other, parts, kinds, after):
+def low_rest(activations, mine, other, groups, after):
     rank = mine.shape[0]
     tokens, units = activations.shape
     rows = units // (lax.axis_size("dp") * CHUNKS)
+    parts = [part for _, _, blocks in groups for part in blocks]
 
     def kernel(mine_ref, other_ref, act_hbm, after_ref, *rest):
         held, sems = rest[-2:]
         copies = blocks_of(act_hbm, held, sems, parts, rows)
-        for place, copy in enumerate(copies):
-            copy.wait()
-            rest[place][...] = term(mine_ref, other_ref, held[place]).astype(kinds[place])
-
+        place = 0
+        for out_ref, (kind, _, blocks) in zip(rest, groups):
+            for row in range(len(blocks)):
+                copies[place].wait()
+                out_ref[row * rows : (row + 1) * rows, :] = term(
+                    mine_ref, other_ref, held[place]
+                ).astype(kind)
+                place += 1
+
+    shapes = [(len(blocks) * rows, rank) for _, _, blocks in groups]
     return pl.pallas_call(
         kernel,
         grid=(1,),
         in_specs=[pl.BlockSpec(memory_space=pltpu.VMEM)] * 2
         + [pl.BlockSpec(memory_space=pltpu.HBM), pl.BlockSpec(memory_space=pl.ANY)],
-        out_specs=[pl.BlockSpec((rows, rank), lambda i: (0, 0))] * len(parts),
-        out_shape=[pltpu.HBM((rows, rank), kind) for kind in kinds],
+        out_specs=[pl.BlockSpec(shape, lambda i: (0, 0)) for shape in shapes],
+        out_shape=[memory(shape, kind) for shape, (kind, memory, _) in zip(shapes, groups)],
         scratch_shapes=[
             pltpu.VMEM((len(parts), tokens, rows), jnp.bfloat16),
             pltpu.SemaphoreType.DMA((len(parts),)),
@@ -187,7 +238,7 @@
 
 
 def adam(own, near, far, first, second, chunk, before, after=()):
-    rows, rank = own.shape
+    rows, rank = far.shape
     tile = rows // 2
     first_fix = 1.0 - 0.9**STEP
     second_fix = 1.0 - 0.999**STEP
@@ -213,7 +264,7 @@
     return pl.pallas_call(
         kernel,
         grid=(2,),
-        in_specs=[local, local, local, whole, whole]
+        in_specs=[whole, local, local, whole, whole]
         + [pl.BlockSpec(memory_space=pl.ANY)] * (len(extra) + len(after)),
         out_specs=[local, whole, whole],
         out_shape=[
@@ -228,50 +279,60 @@
     )(own, near, far, first, second, *extra, *after)
 
 
-def expand(place, normed, basis_cols, bit, chunk, shape, before):
-    rows, rank = normed.shape
+def expand(place, basis_cols, shape, before, pieces):
+    rows, rank = pieces[0][0].shape
     width = basis_cols.shape[0]
     steps = 2
     tile = rows // steps
-
-    def kernel(s, normed_ref, basis_ref, *rest):
+    count = len(pieces)
+
+    def block(i, s):
+        place = jnp.int32(0)
+        for turn, (_, bit, chunk) in enumerate(pieces):
+            here = ((s[0] ^ bit) * CHUNKS + chunk) * steps + i - turn * steps
+            place = here if turn == 0 else jnp.where(i >= turn * steps, here, place)
+        return place, 0
+
+    def kernel(s, basis_ref, *rest):
         out_ref, token_ref = rest[-2:]
-        product = lax.dot_general(
-            normed_ref[...],
-            basis_ref[...],
-            (((1,), (1,)), ((), ())),
-            preferred_element_type=jnp.float32,
-        )
-        out_ref[...] = (0.25 * product).astype(jnp.bfloat16)
+        step = pl.program_id(0)
+        for turn in range(count):
+
+            @pl.when(step // steps == turn)
+            def _():
+                product = lax.dot_general(
+                    rest[turn][...],
+                    basis_ref[...],
+                    (((1,), (1,)), ((), ())),
+                    preferred_element_type=jnp.float32,
+                )
+                out_ref[...] = (0.25 * product).astype(jnp.bfloat16)
+
         token_ref[...] = jnp.zeros_like(token_ref)
+
+    def rows_of(turn):
+        return lambda i, s: (jnp.clip(i - turn * steps, 0, steps - 1), 0)
 
     extra = [] if before is None else [before]
     return pl.pallas_call(
         kernel,
         grid_spec=pltpu.PrefetchScalarGridSpec(
             num_scalar_prefetch=1,
-            grid=(steps,),
-            in_specs=[
-                pl.BlockSpec((tile, rank), lambda i, s: (i, 0)),
-                pl.BlockSpec((width, rank), lambda i, s: (0, 0)),
-            ]
+            grid=(count * steps,),
+            in_specs=[pl.BlockSpec((width, rank), lambda i, s: (0, 0))]
+            + [pl.BlockSpec((tile, rank), rows_of(turn)) for turn in range(count)]
             + [pl.BlockSpec(memory_space=pl.ANY)] * len(extra),
             out_specs=[
-                pl.BlockSpec(
-                    (tile, width), lambda i, s: (((s[0] ^ bit) * CHUNKS + chunk) * steps + i, 0)
-                ),
+                pl.BlockSpec((tile, width), block),
                 pl.BlockSpec((8, 128), lambda i, s: (0, 0)),
             ],
         ),
-        out_shape=[
-            jax.ShapeDtypeStruct(shape, jnp.bfloat16),
-            TOKEN,
-        ],
-        input_output_aliases={3: 0} if extra else {},
-        compiler_params=pltpu.CompilerParams(vmem_limit_bytes=VMEM),
-        cost_estimate=cost(60 * rows * rank * width, 60 * rows * width),
+        out_shape=[jax.ShapeDtypeStruct(shape, jnp.bfloat16), TOKEN],
+        input_output_aliases={2 + count: 0} if extra else {},
+        compiler_params=pltpu.CompilerParams(vmem_limit_bytes=VMEM),
+        cost_estimate=cost(60 * rows * rank * width * count, 60 * rows * width * count),
         name="expand",
-    )(place, normed, basis_cols, *extra)
+    )(place, basis_cols, *[piece for piece, _, _ in pieces], *extra)
 
 
 def paired(activations, out_grad, basis, first_moment, second_moment):
@@ -280,49 +341,59 @@
     width = basis.shape[0] // lax.axis_size("dp")
     fixed = functools.partial(pltpu.with_memory_space_constraint, memory_space=pltpu.HBM)
     shape = (activations.shape[1], width)
-    basis_cols = lax.dynamic_slice_in_dim(basis, z * width, width, 0)
-
-    give, keep = project(fixed(out_grad), fixed(basis))
-    activations = fixed(activations)
-    held, token = load(activations, ((3, 0), (1, 0)), keep)
+    out_grad, activations, basis = fixed(out_grad), fixed(activations), fixed(basis)
+    give = project(out_grad, basis, 0)
+    keep = project(out_grad, basis, 1, (give,))
+    held, basis_cols, token = load(activations, basis, ((3, 0), (3, 1)), keep)
     pair = keep + swap(give, "fsdp", 1)
     mine = settle(pair, swap(pair, "fsdp", 2), token)
     other = swap(mine, "fsdp", 1)
 
     cross_a, token = low_held(held, mine, other, 0, token)
     cross_a = swap(cross_a, "dp", 1)
-    near_a, token = low_held(held, mine, other, 1, token)
-    near_a = swap(near_a, "dp", 1)
-    cross_b, two_a, own_a, two_b, near_b, own_b = low_rest(
+    cross_b, token = low_held(held, mine, other, 1, token)
+    cross_b = swap(cross_b, "dp", 1)
+    plain = jax.ShapeDtypeStruct
+    two_a, near_a, two_b, near_b, own = low_rest(
         activations,
         mine,
         other,
-        ((3, 1), (2, 0), (0, 0), (2, 1), (1, 1), (0, 1)),
-        (b16, f32, f32, f32, b16, f32),
+        (
+            (f32, plain, ((2, 0),)),
+            (b16, plain, ((1, 0),)),
+            (f32, plain, ((2, 1),)),
+            (b16, plain, ((1, 1),)),
+            (f32, pltpu.HBM, ((0, 0), (0, 1))),
+        ),
         token,
     )
-    cross_b, near_b = swap(cross_b, "dp", 1), swap(near_b, "dp", 1)
-    sum_a = swap((two_a + cross_a).astype(b16), "dp", 2)
-    sum_b = swap((two_b + cross_b).astype(b16), "dp", 2)
-
-    first_moment, second_moment = fixed(first_moment), fixed(second_moment)
-    grow = functools.partial(expand, z[None])
-    rows_a, *moments = adam(fixed(own_a), near_a, sum_a, first_moment, second_moment, 0, None)
+    sum_a, near_a = merge(two_a, cross_a, near_a)
+    sum_a = swap(sum_a, "dp", 2)
+    near_a = swap(near_a, "dp", 1)
+    sum_b, near_b = merge(two_b, cross_b, near_b)
+    sum_b = swap(sum_b, "dp", 2)
+    near_b = swap(near_b, "dp", 1)
+
+    first_moment, second_moment, own = fixed(first_moment), fixed(second_moment), fixed(own)
+    grow = functools.partial(expand, z[None], basis_cols, shape)
+    rows_a, *moments = adam(own, near_a, sum_a, first_moment, second_moment, 0, None)
     far_a = swap(rows_a, "dp", 2)
     next_a = swap(rows_a, "dp", 1)
-    update, token = grow(rows_a, basis_cols, 0, 0, shape, None)
+    update, token = grow(None, ((rows_a, 0, 0),))
     rows_b, *moments = adam(
-        fixed(own_b), near_b, sum_b, first_moment, second_moment, 1, moments, (token,)
+        own, near_b, sum_b, first_moment, second_moment, 1, moments, (token,)
     )
     far_b = swap(rows_b, "dp", 2)
     next_b = swap(rows_b, "dp", 1)
-    last_a = swap(far_a, "dp", 1)
-    update, token = grow(next_a, basis_cols, 1, 0, shape, update)
-    update, token = grow(far_a, basis_cols, 2, 0, shape, update)
-    update, token = grow(rows_b, basis_cols, 0, 1, shape, update)
-    last_b = swap(far_b, "dp", 1)
-    for bit, chunk, rows in ((3, 0, last_a), (1, 1, next_b), (2, 1, far_b), (3, 1, last_b)):
-        update, token = grow(rows, basis_cols, bit, chunk, shape, update)
+    update, token = grow(update, ((next_a, 1, 0),))
+    last_a = swap(pass_on(far_a, token), "dp", 1)
+    update, token = grow(update, ((far_a, 2, 0), (rows_b, 0, 1)))
+    last_b = swap(pass_on(far_b, token), "dp", 1)
+    for pieces in (
+        ((next_b, 1, 1), (far_b, 2, 1)),
+        ((last_a, 3, 0), (last_b, 3, 1)),
+    ):
+        update, token = grow(update, pieces)
     return (update, *moments)
 
 

time: 90.6 us -> 82.1 us (0.906)
  waiting for transfers between devices: 33 us -> 13.5 us
  starting transfers between devices: 17.2 us -> 32.1 us
  other arithmetic: 2.16 us -> 0.02 us
  local copies, waits for them, and re-layouts: 1.08 us -> 0 us
    ppermute x15, waiting for transfers between devices: 33 us -> 13.5 us  [swap(): return lax.ppermute(value, axis, [(i, i ^ bit) for i in range(n)])]
    ppermute x15, starting transfers between devices: 17.2 us -> 32.1 us  [swap(): return lax.ppermute(value, axis, [(i, i ^ bit) for i in range(n)])]
    convert_element_type x2 -> x0, other arithmetic: 2.14 us -> none  [the longest x1 1.08 us: paired(): sum_a = swap((two_a + cross_a).astype(b16), 'dp', 2)]
    pallas_call x8 -> x5, Pallas kernels: 20.2 us -> 18.4 us  [expand(): pl.pallas_call(kernel, grid_spec=pltpu.PrefetchScalarGridSpec(num_scalar_...]
    dynamic_slice x1 -> x0, local copies, waits for them, and re-layouts: 1.08 us -> none  [paired(): basis_cols = lax.dynamic_slice_in_dim(basis, z * width, width, 0)]
    pallas_call x1 -> x2, Pallas kernels: 3.64 us -> 4.39 us  [project(): pl.pallas_call(kernel, in_specs=[pl.BlockSpec(memory_space=pltpu.HBM)] *...]
    pallas_call x3 -> x7, Pallas kernels: 6.29 us -> 6.63 us  [the longest x2 4.54 us: adam(): pl.pallas_call(kernel, grid=(2,), in_specs=[whole, local, local, whole, w...]
  transfers between devices with their start and end apart: 15 -> 15, of which waited for: 7 -> 7; matrix products, arithmetic and copies ran while one was open for 4% -> 0% of each run, Pallas kernels for 33% -> 35%
where the time goes in v2:
time: 82.1 us; the launch traced here: 81.9 us
  Pallas kernels  35.6 us (43%)
  starting transfers between devices  32.1 us (39%)
  waiting for transfers between devices  13.5 us (16%)
    ppermute x15, starting transfers between devices, swap(): return lax.ppermute(value, axis, [(i, i ^ bit) for i in range(n)])  32.1 us
    pallas_call x5, Pallas kernels, expand(): pl.pallas_call(kernel, grid_spec=pltpu.PrefetchScalarGridSpec(num_scalar_...  18.4 us
    ppermute x15, waiting for transfers between devices, swap(): return lax.ppermute(value, axis, [(i, i ^ bit) for i in range(n)])  13.5 us
    pallas_call x1, Pallas kernels, low_rest(): pl.pallas_call(kernel, grid=(1,), in_specs=[pl.BlockSpec(memory_space=plt...  5.19 us
    pallas_call x2, Pallas kernels, adam(): pl.pallas_call(kernel, grid=(2,), in_specs=[whole, local, local, whole, w...  4.54 us
    pallas_call x2, Pallas kernels, project(): pl.pallas_call(kernel, in_specs=[pl.BlockSpec(memory_space=pltpu.HBM)] *...  4.39 us
    pallas_call x1, Pallas kernels, load(): pl.pallas_call(kernel, in_specs=[pl.BlockSpec(memory_space=pltpu.HBM)] *...  1.95 us
  transfers between devices with their start and end apart: 15, of which 7 were waited for; matrix products, arithmetic and copies ran while one was open for 0% of the time, Pallas kernels for 35%

profile of v2, /device:TPU:0, one launch (start us, length us, event | category | flops | bytes accessed | tf_op | source)
XLA Modules:
  0.0 81.9 jit_solution(15708381204811152047)
XLA Ops:
  0.6 2.2 %project.2.rest_0_ = f32[128,384]{1,0:T(8,128)S(1)} custom-call(bf16[768,2048]{1,0:T(8,128)(2,1)} %grad_hbm.3, bf16[8192,128]{1,0:T(8,128)(2,1)} %basis_hbm.5), custom_call_target="tpu_custom_call" | custom-call | flops 1000 | bytes 1000 | tf_op jit(solution)/shard_map/project/pallas_call | solution.py:60
  2.8 0.5 collective-permute-start
  3.4 2.2 %project.3.after_ref = f32[128,384]{1,0:T(8,128)S(1)} custom-call(bf16[768,2048]{1,0:T(8,128)(2,1)} %grad_hbm.3, bf16[8192,128]{1,0:T(8,128)(2,1)} %basis_hbm.5, f32[128,384]{1,0:T(8,128)S(1)} %project.2.rest_0_), custom_call_target="tpu_custom_call" | custom-call | flops 1000 | bytes 1000 | tf_op jit(solution)/shard_map/project/pallas_call | solution.py:60
  5.6 0.0 collective-permute-done
  5.6 2.6 %collective-permute-start.1 = (f32[128,384]{1,0:T(8,128)S(1)}, f32[128,384]{1,0:T(8,128)S(1)}, u32[]{:S(2)}, u32[]{:S(2)}) collective-permute-start(f32[128,384]{1,0:T(8,128)S(1)} %add.3.pair_ref), channel_id=1, source_target_pairs={{0,2},{1,3},{2,0},{3,1},{4,6},{5,7},{6,4},{7,5},{8,10},{9,11},{10,... | collective-permute-start | bytes 589832 | tf_op jit(solution)/shard_map/ppermute | solution.py:24
  8.2 2.0 %load.1 = (bf16[2,768,896]{2,1,0:T(8,128)(2,1)S(1)}, bf16[2048,128]{1,0:T(8,128)(2,1)S(1)}, f32[8,128]{1,0:T(8,128)S(1)}) custom-call(bf16[768,7168]{1,0:T(8,128)(2,1)} %act_hbm.3, bf16[8192,128]{1,0:T(8,128)(2,1)} %basis_hbm.5, f32[128,384]{1,0:T(8,128)S(1)} %project.3.after_ref), custom_call_target="tpu_custom_call" | custom-call | bytes 2752512 | tf_op jit(solution)/shard_map/load/pallas_call | solution.py:159
  10.1 3.6 %collective-permute-done.1.far_ref = f32[128,384]{1,0:T(8,128)S(1)} collective-permute-done((f32[128,384]{1,0:T(8,128)S(1)}, f32[128,384]{1,0:T(8,128)S(1)}, u32[]{:S(2)}, u32[]{:S(2)}) %collective-permute-start.1) | collective-permute-done | bytes 196640 | tf_op jit(solution)/shard_map/ppermute | solution.py:24
  13.7 0.1 collective-permute-start.2
  13.8 1.3 %collective-permute-done.2.other_ref = bf16[128,384]{1,0:T(8,128)(2,1)S(1)} collective-permute-done((bf16[128,384]{1,0:T(8,128)(2,1)S(1)}, bf16[128,384]{1,0:T(8,128)(2,1)S(1)}, u32[]{:S(2)}, u32[]{:S(2)}) %collective-permute-start.2) | collective-permute-done | bytes 98336 | tf_op jit(solution)/shard_map/ppermute | solution.py:24
  15.1 0.5 low_held.2
  15.6 1.9 %collective-permute-start.3 = (bf16[896,128]{1,0:T(8,128)(2,1)S(1)}, bf16[896,128]{1,0:T(8,128)(2,1)S(1)}, u32[]{:S(2)}, u32[]{:S(2)}) collective-permute-start(bf16[896,128]{1,0:T(8,128)(2,1)S(1)} %get-tuple-element.40), channel_id=1, source_target_pairs={{0,4},{4,0},{8,12},{12,8},{1,5},{5,1},{9,13},{13,9},{2,6},{6,2},{1... | collective-permute-start | bytes 688136 | tf_op jit(solution)/shard_map/ppermute | solution.py:24
  17.5 0.5 low_held.3
  17.9 0.3 collective-permute-start.9
  18.2 5.2 %low_rest.1 = (f32[896,128]{1,0:T(8,128)S(1)}, bf16[896,128]{1,0:T(8,128)(2,1)S(1)}, f32[896,128]{1,0:T(8,128)S(1)}, bf16[896,128]{1,0:T(8,128)(2,1)S(1)}, f32[1792,128]{1,0:T(8,128)}) custom-call(bf16[128,384]{1,0:T(8,128)(2,1)S(1)} %settle.1.mine_ref, bf16[128,384]{1,0:T(8,128)(2,1)S(1)} %collective-permute-done.2.other_ref, bf16[768,7168]{1,0:T(8,128)(2,1)} %act_hbm.3, ...), custom_call_target="tpu_custom_call" | custom-call | flops 1000 | bytes 1000 | tf_op jit(solution)/shard_map/low_rest/pallas_call | solution.py:223
  23.4 0.7 collective-permute-done.3.got_ref
  24.1 0.1 merge.2
  24.1 1.9 %collective-permute-start.4 = (bf16[896,128]{1,0:T(8,128)(2,1)S(1)}, bf16[896,128]{1,0:T(8,128)(2,1)S(1)}, u32[]{:S(2)}, u32[]{:S(2)}) collective-permute-start(bf16[896,128]{1,0:T(8,128)(2,1)S(1)} %get-tuple-element.42), channel_id=1, source_target_pairs={{0,4},{4,0},{8,12},{12,8},{1,5},{5,1},{9,13},{13,9},{2,6},{6,2},{1... | collective-permute-start | bytes 688136 | tf_op jit(solution)/shard_map/ppermute | solution.py:24
  26.0 2.6 %collective-permute-start.5 = (bf16[896,128]{1,0:T(8,128)(2,1)S(1)}, bf16[896,128]{1,0:T(8,128)(2,1)S(1)}, u32[]{:S(2)}, u32[]{:S(2)}) collective-permute-start(bf16[896,128]{1,0:T(8,128)(2,1)S(1)} %get-tuple-element.43), channel_id=1, source_target_pairs={{0,8},{4,12},{8,0},{12,4},{1,9},{5,13},{9,1},{13,5},{2,10},{6,14},... | collective-permute-start | bytes 688136 | tf_op jit(solution)/shard_map/ppermute | solution.py:24
  28.6 5.3 %collective-permute-done.9.got_ref = bf16[896,128]{1,0:T(8,128)(2,1)S(1)} collective-permute-done((bf16[896,128]{1,0:T(8,128)(2,1)S(1)}, bf16[896,128]{1,0:T(8,128)(2,1)S(1)}, u32[]{:S(2)}, u32[]{:S(2)}) %collective-permute-start.9) | collective-permute-done | bytes 229408 | tf_op jit(solution)/shard_map/ppermute | solution.py:24
  34.0 0.1 collective-permute-start.10
  34.0 4.4 %collective-permute-start.11 = (bf16[896,128]{1,0:T(8,128)(2,1)S(1)}, bf16[896,128]{1,0:T(8,128)(2,1)S(1)}, u32[]{:S(2)}, u32[]{:S(2)}) collective-permute-start(bf16[896,128]{1,0:T(8,128)(2,1)S(1)} %get-tuple-element.51), channel_id=1, source_target_pairs={{0,8},{4,12},{8,0},{12,4},{1,9},{5,13},{9,1},{13,5},{2,10},{6,14},... | collective-permute-start | bytes 688136 | tf_op jit(solution)/shard_map/ppermute | solution.py:24
  38.5 0.5 collective-permute-done.4.near_ref
  38.9 0.0 collective-permute-done.5.far_ref
  38.9 2.3 %adam.2 = (bf16[896,128]{1,0:T(8,128)(2,1)S(1)}, f32[1792,128]{1,0:T(8,128)}, f32[1792,128]{1,0:T(8,128)}) custom-call(f32[1792,128]{1,0:T(8,128)} %get-tuple-element.38.own_ref, bf16[896,128]{1,0:T(8,128)(2,1)S(1)} %collective-permute-done.4.near_ref, bf16[896,128]{1,0:T(8,128)(2,1)S(1)} %collective-permute-done.5.far_ref, f32[1792,128]{1,0:T(8,128)} %first_ref.3, ...), custom_call_target="tpu_custom_call" | custom-call | flops 3440640 | bytes 2752512 | tf_op jit(solution)/shard_map/adam/pallas_call | solution.py:264
  41.2 2.8 %collective-permute-start.7 = (bf16[896,128]{1,0:T(8,128)(2,1)S(1)}, bf16[896,128]{1,0:T(8,128)(2,1)S(1)}, u32[]{:S(2)}, u32[]{:S(2)}) collective-permute-start(bf16[896,128]{1,0:T(8,128)(2,1)S(1)} %get-tuple-element.44.rest_0_), channel_id=1, source_target_pairs={{0,4},{4,0},{8,12},{12,8},{1,5},{5,1},{9,13},{13,9},{2,6},{6,2},{1... | collective-permute-start | bytes 688136 | tf_op jit(solution)/shard_map/ppermute | solution.py:24
  44.0 6.5 %collective-permute-start.6 = (bf16[896,128]{1,0:T(8,128)(2,1)S(1)}, bf16[896,128]{1,0:T(8,128)(2,1)S(1)}, u32[]{:S(2)}, u32[]{:S(2)}) collective-permute-start(bf16[896,128]{1,0:T(8,128)(2,1)S(1)} %get-tuple-element.44.rest_0_), channel_id=1, source_target_pairs={{0,8},{4,12},{8,0},{12,4},{1,9},{5,13},{9,1},{13,5},{2,10},{6,14},... | collective-permute-start | bytes 688136 | tf_op jit(solution)/shard_map/ppermute | solution.py:24
  50.5 2.5 %expand.5 = (bf16[7168,2048]{1,0:T(8,128)(2,1)}, f32[8,128]{1,0:T(8,128)S(1)}) custom-call(s32[1]{0:T(128)} %bitcast.s, bf16[2048,128]{1,0:T(8,128)(2,1)S(1)} %get-tuple-element.33.basis_ref, bf16[896,128]{1,0:T(8,128)(2,1)S(1)} %get-tuple-element.44.rest_0_), custom_call_target="tpu_custom_call" | custom-call | flops 14092861440 | bytes 110100480 | tf_op jit(solution)/shard_map/expand/pallas_call | solution.py:317
  53.0 0.0 collective-permute-done.10.near_ref
  53.0 0.0 collective-permute-done.11.far_ref
  53.0 2.3 %adam.3 = (bf16[896,128]{1,0:T(8,128)(2,1)S(1)}, f32[1792,128]{1,0:T(8,128)}, f32[1792,128]{1,0:T(8,128)}) custom-call(f32[1792,128]{1,0:T(8,128)} %get-tuple-element.38.own_ref, bf16[896,128]{1,0:T(8,128)(2,1)S(1)} %collective-permute-done.10.near_ref, ...), custom_call_target="tpu_custom_call", output_to_operand_aliasing={{1}: (5, {}), {2}: (6, {})} | custom-call | flops 3440640 | bytes 2752512 | tf_op jit(solution)/shard_map/adam/pallas_call | solution.py:264
  55.3 0.0 collective-permute-start.14
  55.3 4.3 %collective-permute-start.12 = (bf16[896,128]{1,0:T(8,128)(2,1)S(1)}, bf16[896,128]{1,0:T(8,128)(2,1)S(1)}, u32[]{:S(2)}, u32[]{:S(2)}) collective-permute-start(bf16[896,128]{1,0:T(8,128)(2,1)S(1)} %get-tuple-element.55.rest_1_), channel_id=1, source_target_pairs={{0,8},{4,12},{8,0},{12,4},{1,9},{5,13},{9,1},{13,5},{2,10},{6,14},... | collective-permute-start | bytes 688136 | tf_op jit(solution)/shard_map/ppermute | solution.py:24
  59.7 0.0 collective-permute-done.7.rest_0_
  59.7 2.5 %expand.6 = (bf16[7168,2048]{1,0:T(8,128)(2,1)}, f32[8,128]{1,0:T(8,128)S(1)}) custom-call(s32[1]{0:T(128)} %bitcast.s, bf16[2048,128]{1,0:T(8,128)(2,1)S(1)} %get-tuple-element.33.basis_ref, bf16[896,128]{1,0:T(8,128)(2,1)S(1)} %collective-permute-done.7.rest_0_, bf16[7168,2048]{1,0:T(8,128)(2,1)} %get-tuple-element.45.rest_1_), custom_call_target="tpu_custom_call", output_to_operand_aliasing={{0}: (3, {})} | custom-call | flops 14092861440 | bytes 110100480 | tf_op jit(solution)/shard_map/expand/pallas_call | solution.py:317
  62.2 0.0 collective-permute-done.6.value_ref.rest_0_
  62.2 0.1 collective-permute-start.8
  62.3 4.5 %expand.7 = (bf16[7168,2048]{1,0:T(8,128)(2,1)}, f32[8,128]{1,0:T(8,128)S(1)}) custom-call(s32[1]{0:T(128)} %bitcast.s, bf16[2048,128]{1,0:T(8,128)(2,1)S(1)} %get-tuple-element.33.basis_ref, bf16[896,128]{1,0:T(8,128)(2,1)S(1)} %collective-permute-done.6.value_ref.rest_0_, ...), custom_call_target="tpu_custom_call", output_to_operand_aliasing={{0}: (4, {})} | custom-call | flops 28185722880 | bytes 220200960 | tf_op jit(solution)/shard_map/expand/pallas_call | solution.py:317
  66.8 1.0 %collective-permute-done.12.value_ref.rest_1_ = bf16[896,128]{1,0:T(8,128)(2,1)S(1)} collective-permute-done((bf16[896,128]{1,0:T(8,128)(2,1)S(1)}, bf16[896,128]{1,0:T(8,128)(2,1)S(1)}, u32[]{:S(2)}, u32[]{:S(2)}) %collective-permute-start.12) | collective-permute-done | bytes 229408 | tf_op jit(solution)/shard_map/ppermute | solution.py:24
  67.8 4.0 %collective-permute-start.13 = (bf16[896,128]{1,0:T(8,128)(2,1)S(1)}, bf16[896,128]{1,0:T(8,128)(2,1)S(1)}, u32[]{:S(2)}, u32[]{:S(2)}) collective-permute-start(bf16[896,128]{1,0:T(8,128)(2,1)S(1)} %pass_on.3), channel_id=1, source_target_pairs={{0,4},{4,0},{8,12},{12,8},{1,5},{5,1},{9,13},{13,9},{2,6},{6,2},{1... | collective-permute-start | bytes 688136 | tf_op jit(solution)/shard_map/ppermute | solution.py:24
  71.9 0.0 collective-permute-done.14.rest_0_
  71.9 4.4 %expand.8 = (bf16[7168,2048]{1,0:T(8,128)(2,1)}, f32[8,128]{1,0:T(8,128)}) custom-call(s32[1]{0:T(128)} %bitcast.s, bf16[2048,128]{1,0:T(8,128)(2,1)S(1)} %get-tuple-element.33.basis_ref, bf16[896,128]{1,0:T(8,128)(2,1)S(1)} %collective-permute-done.14.rest_0_, ...), custom_call_target="tpu_custom_call", output_to_operand_aliasing={{0}: (4, {})} | custom-call | flops 28185722880 | bytes 220200960 | tf_op jit(solution)/shard_map/expand/pallas_call | solution.py:317
  76.3 0.0 collective-permute-done.8.rest_0_
  76.3 1.1 %collective-permute-done.13.rest_1_ = bf16[896,128]{1,0:T(8,128)(2,1)S(1)} collective-permute-done((bf16[896,128]{1,0:T(8,128)(2,1)S(1)}, bf16[896,128]{1,0:T(8,128)(2,1)S(1)}, u32[]{:S(2)}, u32[]{:S(2)}) %collective-permute-start.13) | collective-permute-done | bytes 229408 | tf_op jit(solution)/shard_map/ppermute | solution.py:24
  77.5 4.4 %expand.9 = (bf16[7168,2048]{1,0:T(8,128)(2,1)}, f32[8,128]{1,0:T(8,128)}) custom-call(s32[1]{0:T(128)} %bitcast.s, bf16[2048,128]{1,0:T(8,128)(2,1)S(1)} %get-tuple-element.33.basis_ref, bf16[896,128]{1,0:T(8,128)(2,1)S(1)} %collective-permute-done.8.rest_0_, bf16[896,128]{1,0:T(8,128)(2,1)S(1)} %collective-permute-done.13.rest_1_, ...), custom_call_target="tpu_custom_call", output_to_operand_aliasing={{0}: (4, {})} | custom-call | flops 28185722880 | bytes 220200960 | tf_op jit(solution)/shard_map/expand/pallas_call | solution.py:317
  (5 shorter events, 0.1 us)
Async XLA Ops:
  2.8 2.7 %collective-permute-start = (f32[128,384]{1,0:T(8,128)S(1)}, f32[128,384]{1,0:T(8,128)S(1)}, u32[]{:S(2)}, u32[]{:S(2)}) collective-permute-start(f32[128,384]{1,0:T(8,128)S(1)} %project.2.rest_0_), channel_id=1, source_target_pairs={{0,1},{1,0},{2,3},{3,2},{4,5},{5,4},{6,7},{7,6},{8,9},{9,8},{10,11... | collective-permute-start | bytes 589832 | tf_op jit(solution)/shard_map/ppermute | solution.py:24
  5.6 8.1 %collective-permute-start.1 = (f32[128,384]{1,0:T(8,128)S(1)}, f32[128,384]{1,0:T(8,128)S(1)}, u32[]{:S(2)}, u32[]{:S(2)}) collective-permute-start(f32[128,384]{1,0:T(8,128)S(1)} %add.3.pair_ref), channel_id=1, source_target_pairs={{0,2},{1,3},{2,0},{3,1},{4,6},{5,7},{6,4},{7,5},{8,10},{9,11},{10,... | collective-permute-start | bytes 589832 | tf_op jit(solution)/shard_map/ppermute | solution.py:24
  13.7 1.4 %collective-permute-start.2 = (bf16[128,384]{1,0:T(8,128)(2,1)S(1)}, bf16[128,384]{1,0:T(8,128)(2,1)S(1)}, u32[]{:S(2)}, u32[]{:S(2)}) collective-permute-start(bf16[128,384]{1,0:T(8,128)(2,1)S(1)} %settle.1.mine_ref), channel_id=1, source_target_pairs={{0,1},{1,0},{2,3},{3,2},{4,5},{5,4},{6,7},{7,6},{8,9},{9,8},{10,11... | collective-permute-start | bytes 294920 | tf_op jit(solution)/shard_map/ppermute | solution.py:24
  15.6 8.5 %collective-permute-start.3 = (bf16[896,128]{1,0:T(8,128)(2,1)S(1)}, bf16[896,128]{1,0:T(8,128)(2,1)S(1)}, u32[]{:S(2)}, u32[]{:S(2)}) collective-permute-start(bf16[896,128]{1,0:T(8,128)(2,1)S(1)} %get-tuple-element.40), channel_id=1, source_target_pairs={{0,4},{4,0},{8,12},{12,8},{1,5},{5,1},{9,13},{13,9},{2,6},{6,2},{1... | collective-permute-start | bytes 688136 | tf_op jit(solution)/shard_map/ppermute | solution.py:24
  17.9 16.0 %collective-permute-start.9 = (bf16[896,128]{1,0:T(8,128)(2,1)S(1)}, bf16[896,128]{1,0:T(8,128)(2,1)S(1)}, u32[]{:S(2)}, u32[]{:S(2)}) collective-permute-start(bf16[896,128]{1,0:T(8,128)(2,1)S(1)} %get-tuple-element.48), channel_id=1, source_target_pairs={{0,4},{4,0},{8,12},{12,8},{1,5},{5,1},{9,13},{13,9},{2,6},{6,2},{1... | collective-permute-start | bytes 688136 | tf_op jit(solution)/shard_map/ppermute | solution.py:24
  24.1 14.8 %collective-permute-start.4 = (bf16[896,128]{1,0:T(8,128)(2,1)S(1)}, bf16[896,128]{1,0:T(8,128)(2,1)S(1)}, u32[]{:S(2)}, u32[]{:S(2)}) collective-permute-start(bf16[896,128]{1,0:T(8,128)(2,1)S(1)} %get-tuple-element.42), channel_id=1, source_target_pairs={{0,4},{4,0},{8,12},{12,8},{1,5},{5,1},{9,13},{13,9},{2,6},{6,2},{1... | collective-permute-start | bytes 688136 | tf_op jit(solution)/shard_map/ppermute | solution.py:24
  26.0 12.9 %collective-permute-start.5 = (bf16[896,128]{1,0:T(8,128)(2,1)S(1)}, bf16[896,128]{1,0:T(8,128)(2,1)S(1)}, u32[]{:S(2)}, u32[]{:S(2)}) collective-permute-start(bf16[896,128]{1,0:T(8,128)(2,1)S(1)} %get-tuple-element.43), channel_id=1, source_target_pairs={{0,8},{4,12},{8,0},{12,4},{1,9},{5,13},{9,1},{13,5},{2,10},{6,14},... | collective-permute-start | bytes 688136 | tf_op jit(solution)/shard_map/ppermute | solution.py:24
  34.0 19.1 %collective-permute-start.10 = (bf16[896,128]{1,0:T(8,128)(2,1)S(1)}, bf16[896,128]{1,0:T(8,128)(2,1)S(1)}, u32[]{:S(2)}, u32[]{:S(2)}) collective-permute-start(bf16[896,128]{1,0:T(8,128)(2,1)S(1)} %get-tuple-element.50), channel_id=1, source_target_pairs={{0,4},{4,0},{8,12},{12,8},{1,5},{5,1},{9,13},{13,9},{2,6},{6,2},{1... | collective-permute-start | bytes 688136 | tf_op jit(solution)/shard_map/ppermute | solution.py:24
  34.0 19.0 %collective-permute-start.11 = (bf16[896,128]{1,0:T(8,128)(2,1)S(1)}, bf16[896,128]{1,0:T(8,128)(2,1)S(1)}, u32[]{:S(2)}, u32[]{:S(2)}) collective-permute-start(bf16[896,128]{1,0:T(8,128)(2,1)S(1)} %get-tuple-element.51), channel_id=1, source_target_pairs={{0,8},{4,12},{8,0},{12,4},{1,9},{5,13},{9,1},{13,5},{2,10},{6,14},... | collective-permute-start | bytes 688136 | tf_op jit(solution)/shard_map/ppermute | solution.py:24
  41.2 18.5 %collective-permute-start.7 = (bf16[896,128]{1,0:T(8,128)(2,1)S(1)}, bf16[896,128]{1,0:T(8,128)(2,1)S(1)}, u32[]{:S(2)}, u32[]{:S(2)}) collective-permute-start(bf16[896,128]{1,0:T(8,128)(2,1)S(1)} %get-tuple-element.44.rest_0_), channel_id=1, source_target_pairs={{0,4},{4,0},{8,12},{12,8},{1,5},{5,1},{9,13},{13,9},{2,6},{6,2},{1... | collective-permute-start | bytes 688136 | tf_op jit(solution)/shard_map/ppermute | solution.py:24
  44.0 18.3 %collective-permute-start.6 = (bf16[896,128]{1,0:T(8,128)(2,1)S(1)}, bf16[896,128]{1,0:T(8,128)(2,1)S(1)}, u32[]{:S(2)}, u32[]{:S(2)}) collective-permute-start(bf16[896,128]{1,0:T(8,128)(2,1)S(1)} %get-tuple-element.44.rest_0_), channel_id=1, source_target_pairs={{0,8},{4,12},{8,0},{12,4},{1,9},{5,13},{9,1},{13,5},{2,10},{6,14},... | collective-permute-start | bytes 688136 | tf_op jit(solution)/shard_map/ppermute | solution.py:24
  55.3 16.6 %collective-permute-start.14 = (bf16[896,128]{1,0:T(8,128)(2,1)S(1)}, bf16[896,128]{1,0:T(8,128)(2,1)S(1)}, u32[]{:S(2)}, u32[]{:S(2)}) collective-permute-start(bf16[896,128]{1,0:T(8,128)(2,1)S(1)} %get-tuple-element.55.rest_1_), channel_id=1, source_target_pairs={{0,4},{4,0},{8,12},{12,8},{1,5},{5,1},{9,13},{13,9},{2,6},{6,2},{1... | collective-permute-start | bytes 688136 | tf_op jit(solution)/shard_map/ppermute | solution.py:24
  55.3 12.5 %collective-permute-start.12 = (bf16[896,128]{1,0:T(8,128)(2,1)S(1)}, bf16[896,128]{1,0:T(8,128)(2,1)S(1)}, u32[]{:S(2)}, u32[]{:S(2)}) collective-permute-start(bf16[896,128]{1,0:T(8,128)(2,1)S(1)} %get-tuple-element.55.rest_1_), channel_id=1, source_target_pairs={{0,8},{4,12},{8,0},{12,4},{1,9},{5,13},{9,1},{13,5},{2,10},{6,14},... | collective-permute-start | bytes 688136 | tf_op jit(solution)/shard_map/ppermute | solution.py:24
  62.2 14.1 %collective-permute-start.8 = (bf16[896,128]{1,0:T(8,128)(2,1)S(1)}, bf16[896,128]{1,0:T(8,128)(2,1)S(1)}, u32[]{:S(2)}, u32[]{:S(2)}) collective-permute-start(bf16[896,128]{1,0:T(8,128)(2,1)S(1)} %pass_on.2), channel_id=1, source_target_pairs={{0,4},{4,0},{8,12},{12,8},{1,5},{5,1},{9,13},{13,9},{2,6},{6,2},{1... | collective-permute-start | bytes 688136 | tf_op jit(solution)/shard_map/ppermute | solution.py:24
  67.8 9.6 %collective-permute-start.13 = (bf16[896,128]{1,0:T(8,128)(2,1)S(1)}, bf16[896,128]{1,0:T(8,128)(2,1)S(1)}, u32[]{:S(2)}, u32[]{:S(2)}) collective-permute-start(bf16[896,128]{1,0:T(8,128)(2,1)S(1)} %pass_on.3), channel_id=1, source_target_pairs={{0,4},{4,0},{8,12},{12,8},{1,5},{5,1},{9,13},{13,9},{2,6},{6,2},{1... | collective-permute-start | bytes 688136 | tf_op jit(solution)/shard_map/ppermute | solution.py:24

commit v3 on v2

--- a/solution.py
+++ b/solution.py
@@ -24,15 +24,14 @@
     return lax.ppermute(value, axis, [(i, i ^ bit) for i in range(n)])
 
 
-def project(out_grad, basis, turn, after=()):
+def project_give(out_grad, basis):
     tokens, features = out_grad.shape
     rows, rank = tokens // 2, basis.shape[1]
     piece = rows // PIECES
 
-    def kernel(grad_hbm, basis_hbm, *rest):
-        out_ref, grad, base, sems = rest[-4:]
+    def kernel(grad_hbm, basis_hbm, out_ref, held, base, grad, sems):
         place = lax.axis_index("fsdp")
-        half = lax.rem(place + 1 + turn, 2)
+        core = lax.rem(place, 2)
         copies = [
             pltpu.make_async_copy(
                 basis_hbm.at[pl.ds(pl.multiple_of(place * features, features), features), :],
@@ -40,38 +39,62 @@
                 sems.at[0],
             )
         ]
-        for part in range(PIECES):
-            first = half * rows + part * piece
-            copies.append(
-                pltpu.make_async_copy(
-                    grad_hbm.at[pl.ds(pl.multiple_of(first, piece), piece), :],
-                    grad.at[pl.ds(part * piece, piece), :],
-                    sems.at[part + 1],
+        for turn, (half, target) in enumerate(((1 - core, grad), (core, held))):
+            for part in range(PIECES):
+                first = half * rows + part * piece
+                copies.append(
+                    pltpu.make_async_copy(
+                        grad_hbm.at[pl.ds(pl.multiple_of(first, piece), piece), :],
+                        target.at[pl.ds(part * piece, piece), :],
+                        sems.at[turn * PIECES + part + 1],
+                    )
                 )
-            )
         for copy in copies:
             copy.start()
-        for copy in copies:
+        for copy in copies[: PIECES + 1]:
             copy.wait()
         out_ref[...] = jnp.dot(
             grad[...], base[...], preferred_element_type=jnp.float32
         ).T
-
-    return pl.pallas_call(
-        kernel,
-        in_specs=[pl.BlockSpec(memory_space=pltpu.HBM)] * 2
-        + [pl.BlockSpec(memory_space=pl.ANY)] * len(after),
+        for copy in copies[PIECES + 1 :]:
+            copy.wait()
+
+    return pl.pallas_call(
+        kernel,
+        in_specs=[pl.BlockSpec(memory_space=pltpu.HBM)] * 2,
+        out_specs=[pl.BlockSpec(memory_space=pltpu.VMEM)] * 3,
+        out_shape=[
+            jax.ShapeDtypeStruct((rank, rows), jnp.float32),
+            jax.ShapeDtypeStruct((rows, features), jnp.bfloat16),
+            jax.ShapeDtypeStruct((features, rank), jnp.bfloat16),
+        ],
+        scratch_shapes=[
+            pltpu.VMEM((rows, features), jnp.bfloat16),
+            pltpu.SemaphoreType.DMA((2 * PIECES + 1,)),
+        ],
+        compiler_params=pltpu.CompilerParams(vmem_limit_bytes=VMEM),
+        cost_estimate=cost(1000, 1000),
+        name="project_give",
+    )(out_grad, basis)
+
+
+def project_keep(grad, base):
+    rows, rank = grad.shape[0], base.shape[1]
+
+    def kernel(grad_ref, base_ref, out_ref):
+        out_ref[...] = jnp.dot(
+            grad_ref[...], base_ref[...], preferred_element_type=jnp.float32
+        ).T
+
+    return pl.pallas_call(
+        kernel,
+        in_specs=[pl.BlockSpec(memory_space=pltpu.VMEM)] * 2,
         out_specs=pl.BlockSpec(memory_space=pltpu.VMEM),
         out_shape=jax.ShapeDtypeStruct((rank, rows), jnp.float32),
-        scratch_shapes=[
-            pltpu.VMEM((rows, features), jnp.bfloat16),
-            pltpu.VMEM((features, rank), jnp.bfloat16),
-            pltpu.SemaphoreType.DMA((PIECES + 1,)),
-        ],
         compiler_params=pltpu.CompilerParams(vmem_limit_bytes=VMEM),
         cost_estimate=cost(1000, 1000),
-        name="project",
-    )(out_grad, basis, *after)
+        name="project_keep",
+    )(grad, base)
 
 
 def settle(pair, far, after):
@@ -342,8 +365,8 @@
     fixed = functools.partial(pltpu.with_memory_space_constraint, memory_space=pltpu.HBM)
     shape = (activations.shape[1], width)
     out_grad, activations, basis = fixed(out_grad), fixed(activations), fixed(basis)
-    give = project(out_grad, basis, 0)
-    keep = project(out_grad, basis, 1, (give,))
+    give, grad, base = project_give(out_grad, basis)
+    keep = project_keep(grad, base)
     held, basis_cols, token = load(activations, basis, ((3, 0), (3, 1)), keep)
     pair = keep + swap(give, "fsdp", 1)
     mine = settle(pair, swap(pair, "fsdp", 2), token)

time: 82.1 us -> 81 us (0.987)
  Pallas kernels: 35.6 us -> 34.1 us
    pallas_call x2, Pallas kernels: 4.39 us -> 2.87 us  [the longest x1 2.23 us: project_give(): pl.pallas_call(kernel, in_specs=[pl.BlockSpec(memory_space=pltpu.HBM)] *...]
  transfers between devices with their start and end apart: 15 -> 15, of which waited for: 7 -> 8; matrix products, arithmetic and copies ran while one was open for 0% -> 0% of each run, Pallas kernels for 35% -> 33%
where the time goes in v3:
time: 81 us; the launch traced here: 80.8 us
  Pallas kernels  34.1 us (42%)
  starting transfers between devices  32.4 us (40%)
  waiting for transfers between devices  13.6 us (17%)
    ppermute x15, starting transfers between devices, swap(): return lax.ppermute(value, axis, [(i, i ^ bit) for i in range(n)])  32.4 us
    pallas_call x5, Pallas kernels, expand(): pl.pallas_call(kernel, grid_spec=pltpu.PrefetchScalarGridSpec(num_scalar_...  18.4 us
    ppermute x15, waiting for transfers between devices, swap(): return lax.ppermute(value, axis, [(i, i ^ bit) for i in range(n)])  13.6 us
    pallas_call x1, Pallas kernels, low_rest(): pl.pallas_call(kernel, grid=(1,), in_specs=[pl.BlockSpec(memory_space=plt...  5.2 us
    pallas_call x2, Pallas kernels, adam(): pl.pallas_call(kernel, grid=(2,), in_specs=[whole, local, local, whole, w...  4.54 us
    pallas_call x1, Pallas kernels, project_give(): pl.pallas_call(kernel, in_specs=[pl.BlockSpec(memory_space=pltpu.HBM)] *...  2.23 us
    pallas_call x1, Pallas kernels, load(): pl.pallas_call(kernel, in_specs=[pl.BlockSpec(memory_space=pltpu.HBM)] *...  1.95 us
  transfers between devices with their start and end apart: 15, of which 8 were waited for; matrix products, arithmetic and copies ran while one was open for 0% of the time, Pallas kernels for 33%

profile of v3, /device:TPU:0, one launch (start us, length us, event | category | flops | bytes accessed | tf_op | source)
XLA Modules:
  0.0 80.8 jit_solution(8335419210204114183)
XLA Ops:
  0.6 2.2 %project_give.1 = (f32[128,384]{1,0:T(8,128)S(1)}, bf16[384,2048]{1,0:T(8,128)(2,1)S(1)}, bf16[2048,128]{1,0:T(8,128)(2,1)S(1)}) custom-call(bf16[768,2048]{1,0:T(8,128)(2,1)} %grad_hbm.1, bf16[8192,128]{1,0:T(8,128)(2,1)} %basis_hbm.3), custom_call_target="tpu_custom_call" | custom-call | flops 1000 | bytes 1000 | tf_op jit(solution)/shard_map/project_give/pallas_call | solution.py:62
  2.9 0.5 collective-permute-start
  3.4 0.6 project_keep.1.after_ref
  4.0 0.4 collective-permute-done
  4.5 2.9 %collective-permute-start.1 = (f32[128,384]{1,0:T(8,128)S(1)}, f32[128,384]{1,0:T(8,128)S(1)}, u32[]{:S(2)}, u32[]{:S(2)}) collective-permute-start(f32[128,384]{1,0:T(8,128)S(1)} %add.3.pair_ref), channel_id=1, source_target_pairs={{0,2},{1,3},{2,0},{3,1},{4,6},{5,7},{6,4},{7,5},{8,10},{9,11},{10,... | collective-permute-start | bytes 589832 | tf_op jit(solution)/shard_map/ppermute | solution.py:24
  7.4 2.0 %load.1 = (bf16[2,768,896]{2,1,0:T(8,128)(2,1)S(1)}, bf16[2048,128]{1,0:T(8,128)(2,1)S(1)}, f32[8,128]{1,0:T(8,128)S(1)}) custom-call(bf16[768,7168]{1,0:T(8,128)(2,1)} %act_hbm.3, bf16[8192,128]{1,0:T(8,128)(2,1)} %basis_hbm.3, f32[128,384]{1,0:T(8,128)S(1)} %project_keep.1.after_ref), custom_call_target="tpu_custom_call" | custom-call | bytes 2752512 | tf_op jit(solution)/shard_map/load/pallas_call | solution.py:182
  9.4 3.2 %collective-permute-done.1.far_ref = f32[128,384]{1,0:T(8,128)S(1)} collective-permute-done((f32[128,384]{1,0:T(8,128)S(1)}, f32[128,384]{1,0:T(8,128)S(1)}, u32[]{:S(2)}, u32[]{:S(2)}) %collective-permute-start.1) | collective-permute-done | bytes 196640 | tf_op jit(solution)/shard_map/ppermute | solution.py:24
  12.6 0.1 collective-permute-start.2
  12.7 1.3 %collective-permute-done.2.other_ref = bf16[128,384]{1,0:T(8,128)(2,1)S(1)} collective-permute-done((bf16[128,384]{1,0:T(8,128)(2,1)S(1)}, bf16[128,384]{1,0:T(8,128)(2,1)S(1)}, u32[]{:S(2)}, u32[]{:S(2)}) %collective-permute-start.2) | collective-permute-done | bytes 98336 | tf_op jit(solution)/shard_map/ppermute | solution.py:24
  14.0 0.5 low_held.2
  14.5 1.9 %collective-permute-start.3 = (bf16[896,128]{1,0:T(8,128)(2,1)S(1)}, bf16[896,128]{1,0:T(8,128)(2,1)S(1)}, u32[]{:S(2)}, u32[]{:S(2)}) collective-permute-start(bf16[896,128]{1,0:T(8,128)(2,1)S(1)} %get-tuple-element.46), channel_id=1, source_target_pairs={{0,4},{4,0},{8,12},{12,8},{1,5},{5,1},{9,13},{13,9},{2,6},{6,2},{1... | collective-permute-start | bytes 688136 | tf_op jit(solution)/shard_map/ppermute | solution.py:24
  16.4 0.4 low_held.3
  16.8 0.3 collective-permute-start.9
  17.1 5.2 %low_rest.1 = (f32[896,128]{1,0:T(8,128)S(1)}, bf16[896,128]{1,0:T(8,128)(2,1)S(1)}, f32[896,128]{1,0:T(8,128)S(1)}, bf16[896,128]{1,0:T(8,128)(2,1)S(1)}, f32[1792,128]{1,0:T(8,128)}) custom-call(bf16[128,384]{1,0:T(8,128)(2,1)S(1)} %settle.1.mine_ref, bf16[128,384]{1,0:T(8,128)(2,1)S(1)} %collective-permute-done.2.other_ref, bf16[768,7168]{1,0:T(8,128)(2,1)} %act_hbm.3, ...), custom_call_target="tpu_custom_call" | custom-call | flops 1000 | bytes 1000 | tf_op jit(solution)/shard_map/low_rest/pallas_call | solution.py:246
  22.3 0.7 collective-permute-done.3.got_ref
  23.0 0.1 merge.2
  23.0 1.9 %collective-permute-start.4 = (bf16[896,128]{1,0:T(8,128)(2,1)S(1)}, bf16[896,128]{1,0:T(8,128)(2,1)S(1)}, u32[]{:S(2)}, u32[]{:S(2)}) collective-permute-start(bf16[896,128]{1,0:T(8,128)(2,1)S(1)} %get-tuple-element.48), channel_id=1, source_target_pairs={{0,4},{4,0},{8,12},{12,8},{1,5},{5,1},{9,13},{13,9},{2,6},{6,2},{1... | collective-permute-start | bytes 688136 | tf_op jit(solution)/shard_map/ppermute | solution.py:24
  24.9 2.6 %collective-permute-start.5 = (bf16[896,128]{1,0:T(8,128)(2,1)S(1)}, bf16[896,128]{1,0:T(8,128)(2,1)S(1)}, u32[]{:S(2)}, u32[]{:S(2)}) collective-permute-start(bf16[896,128]{1,0:T(8,128)(2,1)S(1)} %get-tuple-element.49), channel_id=1, source_target_pairs={{0,8},{4,12},{8,0},{12,4},{1,9},{5,13},{9,1},{13,5},{2,10},{6,14},... | collective-permute-start | bytes 688136 | tf_op jit(solution)/shard_map/ppermute | solution.py:24
  27.5 5.3 %collective-permute-done.9.got_ref = bf16[896,128]{1,0:T(8,128)(2,1)S(1)} collective-permute-done((bf16[896,128]{1,0:T(8,128)(2,1)S(1)}, bf16[896,128]{1,0:T(8,128)(2,1)S(1)}, u32[]{:S(2)}, u32[]{:S(2)}) %collective-permute-start.9) | collective-permute-done | bytes 229408 | tf_op jit(solution)/shard_map/ppermute | solution.py:24
  32.9 0.1 collective-permute-start.10
  32.9 4.4 %collective-permute-start.11 = (bf16[896,128]{1,0:T(8,128)(2,1)S(1)}, bf16[896,128]{1,0:T(8,128)(2,1)S(1)}, u32[]{:S(2)}, u32[]{:S(2)}) collective-permute-start(bf16[896,128]{1,0:T(8,128)(2,1)S(1)} %get-tuple-element.57), channel_id=1, source_target_pairs={{0,8},{4,12},{8,0},{12,4},{1,9},{5,13},{9,1},{13,5},{2,10},{6,14},... | collective-permute-start | bytes 688136 | tf_op jit(solution)/shard_map/ppermute | solution.py:24
  37.3 0.5 collective-permute-done.4.near_ref
  37.8 0.0 collective-permute-done.5.far_ref
  37.8 2.3 %adam.2 = (bf16[896,128]{1,0:T(8,128)(2,1)S(1)}, f32[1792,128]{1,0:T(8,128)}, f32[1792,128]{1,0:T(8,128)}) custom-call(f32[1792,128]{1,0:T(8,128)} %get-tuple-element.44.own_ref, bf16[896,128]{1,0:T(8,128)(2,1)S(1)} %collective-permute-done.4.near_ref, bf16[896,128]{1,0:T(8,128)(2,1)S(1)} %collective-permute-done.5.far_ref, f32[1792,128]{1,0:T(8,128)} %first_ref.3, ...), custom_call_target="tpu_custom_call" | custom-call | flops 3440640 | bytes 2752512 | tf_op jit(solution)/shard_map/adam/pallas_call | solution.py:287
  40.1 2.8 %collective-permute-start.7 = (bf16[896,128]{1,0:T(8,128)(2,1)S(1)}, bf16[896,128]{1,0:T(8,128)(2,1)S(1)}, u32[]{:S(2)}, u32[]{:S(2)}) collective-permute-start(bf16[896,128]{1,0:T(8,128)(2,1)S(1)} %get-tuple-element.50.rest_0_), channel_id=1, source_target_pairs={{0,4},{4,0},{8,12},{12,8},{1,5},{5,1},{9,13},{13,9},{2,6},{6,2},{1... | collective-permute-start | bytes 688136 | tf_op jit(solution)/shard_map/ppermute | solution.py:24
  42.9 6.5 %collective-permute-start.6 = (bf16[896,128]{1,0:T(8,128)(2,1)S(1)}, bf16[896,128]{1,0:T(8,128)(2,1)S(1)}, u32[]{:S(2)}, u32[]{:S(2)}) collective-permute-start(bf16[896,128]{1,0:T(8,128)(2,1)S(1)} %get-tuple-element.50.rest_0_), channel_id=1, source_target_pairs={{0,8},{4,12},{8,0},{12,4},{1,9},{5,13},{9,1},{13,5},{2,10},{6,14},... | collective-permute-start | bytes 688136 | tf_op jit(solution)/shard_map/ppermute | solution.py:24
  49.4 2.5 %expand.5 = (bf16[7168,2048]{1,0:T(8,128)(2,1)}, f32[8,128]{1,0:T(8,128)S(1)}) custom-call(s32[1]{0:T(128)} %bitcast.s, bf16[2048,128]{1,0:T(8,128)(2,1)S(1)} %get-tuple-element.38.basis_ref, bf16[896,128]{1,0:T(8,128)(2,1)S(1)} %get-tuple-element.50.rest_0_), custom_call_target="tpu_custom_call" | custom-call | flops 14092861440 | bytes 110100480 | tf_op jit(solution)/shard_map/expand/pallas_call | solution.py:340
  51.9 0.0 collective-permute-done.10.near_ref
  51.9 0.0 collective-permute-done.11.far_ref
  51.9 2.3 %adam.3 = (bf16[896,128]{1,0:T(8,128)(2,1)S(1)}, f32[1792,128]{1,0:T(8,128)}, f32[1792,128]{1,0:T(8,128)}) custom-call(f32[1792,128]{1,0:T(8,128)} %get-tuple-element.44.own_ref, bf16[896,128]{1,0:T(8,128)(2,1)S(1)} %collective-permute-done.10.near_ref, ...), custom_call_target="tpu_custom_call", output_to_operand_aliasing={{1}: (5, {}), {2}: (6, {})} | custom-call | flops 3440640 | bytes 2752512 | tf_op jit(solution)/shard_map/adam/pallas_call | solution.py:287
  54.2 0.0 collective-permute-start.14
  54.2 4.3 %collective-permute-start.12 = (bf16[896,128]{1,0:T(8,128)(2,1)S(1)}, bf16[896,128]{1,0:T(8,128)(2,1)S(1)}, u32[]{:S(2)}, u32[]{:S(2)}) collective-permute-start(bf16[896,128]{1,0:T(8,128)(2,1)S(1)} %get-tuple-element.61.rest_1_), channel_id=1, source_target_pairs={{0,8},{4,12},{8,0},{12,4},{1,9},{5,13},{9,1},{13,5},{2,10},{6,14},... | collective-permute-start | bytes 688136 | tf_op jit(solution)/shard_map/ppermute | solution.py:24
  58.5 0.0 collective-permute-done.7.rest_0_
  58.6 2.6 %expand.6 = (bf16[7168,2048]{1,0:T(8,128)(2,1)}, f32[8,128]{1,0:T(8,128)S(1)}) custom-call(s32[1]{0:T(128)} %bitcast.s, bf16[2048,128]{1,0:T(8,128)(2,1)S(1)} %get-tuple-element.38.basis_ref, bf16[896,128]{1,0:T(8,128)(2,1)S(1)} %collective-permute-done.7.rest_0_, bf16[7168,2048]{1,0:T(8,128)(2,1)} %get-tuple-element.51.rest_1_), custom_call_target="tpu_custom_call", output_to_operand_aliasing={{0}: (3, {})} | custom-call | flops 14092861440 | bytes 110100480 | tf_op jit(solution)/shard_map/expand/pallas_call | solution.py:340
  61.1 0.0 collective-permute-done.6.value_ref.rest_0_
  61.1 0.1 collective-permute-start.8
  61.2 4.5 %expand.7 = (bf16[7168,2048]{1,0:T(8,128)(2,1)}, f32[8,128]{1,0:T(8,128)S(1)}) custom-call(s32[1]{0:T(128)} %bitcast.s, bf16[2048,128]{1,0:T(8,128)(2,1)S(1)} %get-tuple-element.38.basis_ref, bf16[896,128]{1,0:T(8,128)(2,1)S(1)} %collective-permute-done.6.value_ref.rest_0_, ...), custom_call_target="tpu_custom_call", output_to_operand_aliasing={{0}: (4, {})} | custom-call | flops 28185722880 | bytes 220200960 | tf_op jit(solution)/shard_map/expand/pallas_call | solution.py:340
  65.7 1.0 %collective-permute-done.12.value_ref.rest_1_ = bf16[896,128]{1,0:T(8,128)(2,1)S(1)} collective-permute-done((bf16[896,128]{1,0:T(8,128)(2,1)S(1)}, bf16[896,128]{1,0:T(8,128)(2,1)S(1)}, u32[]{:S(2)}, u32[]{:S(2)}) %collective-permute-start.12) | collective-permute-done | bytes 229408 | tf_op jit(solution)/shard_map/ppermute | solution.py:24
  66.7 4.0 %collective-permute-start.13 = (bf16[896,128]{1,0:T(8,128)(2,1)S(1)}, bf16[896,128]{1,0:T(8,128)(2,1)S(1)}, u32[]{:S(2)}, u32[]{:S(2)}) collective-permute-start(bf16[896,128]{1,0:T(8,128)(2,1)S(1)} %pass_on.3), channel_id=1, source_target_pairs={{0,4},{4,0},{8,12},{12,8},{1,5},{5,1},{9,13},{13,9},{2,6},{6,2},{1... | collective-permute-start | bytes 688136 | tf_op jit(solution)/shard_map/ppermute | solution.py:24
  70.8 0.0 collective-permute-done.14.rest_0_
  70.8 4.4 %expand.8 = (bf16[7168,2048]{1,0:T(8,128)(2,1)}, f32[8,128]{1,0:T(8,128)}) custom-call(s32[1]{0:T(128)} %bitcast.s, bf16[2048,128]{1,0:T(8,128)(2,1)S(1)} %get-tuple-element.38.basis_ref, bf16[896,128]{1,0:T(8,128)(2,1)S(1)} %collective-permute-done.14.rest_0_, ...), custom_call_target="tpu_custom_call", output_to_operand_aliasing={{0}: (4, {})} | custom-call | flops 28185722880 | bytes 220200960 | tf_op jit(solution)/shard_map/expand/pallas_call | solution.py:340
  75.2 0.0 collective-permute-done.8.rest_0_
  75.2 1.1 %collective-permute-done.13.rest_1_ = bf16[896,128]{1,0:T(8,128)(2,1)S(1)} collective-permute-done((bf16[896,128]{1,0:T(8,128)(2,1)S(1)}, bf16[896,128]{1,0:T(8,128)(2,1)S(1)}, u32[]{:S(2)}, u32[]{:S(2)}) %collective-permute-start.13) | collective-permute-done | bytes 229408 | tf_op jit(solution)/shard_map/ppermute | solution.py:24
  76.4 4.4 %expand.9 = (bf16[7168,2048]{1,0:T(8,128)(2,1)}, f32[8,128]{1,0:T(8,128)}) custom-call(s32[1]{0:T(128)} %bitcast.s, bf16[2048,128]{1,0:T(8,128)(2,1)S(1)} %get-tuple-element.38.basis_ref, bf16[896,128]{1,0:T(8,128)(2,1)S(1)} %collective-permute-done.8.rest_0_, bf16[896,128]{1,0:T(8,128)(2,1)S(1)} %collective-permute-done.13.rest_1_, ...), custom_call_target="tpu_custom_call", output_to_operand_aliasing={{0}: (4, {})} | custom-call | flops 28185722880 | bytes 220200960 | tf_op jit(solution)/shard_map/expand/pallas_call | solution.py:340
  (5 shorter events, 0.1 us)
Async XLA Ops:
  2.9 1.6 %collective-permute-start = (f32[128,384]{1,0:T(8,128)S(1)}, f32[128,384]{1,0:T(8,128)S(1)}, u32[]{:S(2)}, u32[]{:S(2)}) collective-permute-start(f32[128,384]{1,0:T(8,128)S(1)} %get-tuple-element.39), channel_id=1, source_target_pairs={{0,1},{1,0},{2,3},{3,2},{4,5},{5,4},{6,7},{7,6},{8,9},{9,8},{10,11... | collective-permute-start | bytes 589832 | tf_op jit(solution)/shard_map/ppermute | solution.py:24
  4.5 8.1 %collective-permute-start.1 = (f32[128,384]{1,0:T(8,128)S(1)}, f32[128,384]{1,0:T(8,128)S(1)}, u32[]{:S(2)}, u32[]{:S(2)}) collective-permute-start(f32[128,384]{1,0:T(8,128)S(1)} %add.3.pair_ref), channel_id=1, source_target_pairs={{0,2},{1,3},{2,0},{3,1},{4,6},{5,7},{6,4},{7,5},{8,10},{9,11},{10,... | collective-permute-start | bytes 589832 | tf_op jit(solution)/shard_map/ppermute | solution.py:24
  12.6 1.4 %collective-permute-start.2 = (bf16[128,384]{1,0:T(8,128)(2,1)S(1)}, bf16[128,384]{1,0:T(8,128)(2,1)S(1)}, u32[]{:S(2)}, u32[]{:S(2)}) collective-permute-start(bf16[128,384]{1,0:T(8,128)(2,1)S(1)} %settle.1.mine_ref), channel_id=1, source_target_pairs={{0,1},{1,0},{2,3},{3,2},{4,5},{5,4},{6,7},{7,6},{8,9},{9,8},{10,11... | collective-permute-start | bytes 294920 | tf_op jit(solution)/shard_map/ppermute | solution.py:24
  14.5 8.5 %collective-permute-start.3 = (bf16[896,128]{1,0:T(8,128)(2,1)S(1)}, bf16[896,128]{1,0:T(8,128)(2,1)S(1)}, u32[]{:S(2)}, u32[]{:S(2)}) collective-permute-start(bf16[896,128]{1,0:T(8,128)(2,1)S(1)} %get-tuple-element.46), channel_id=1, source_target_pairs={{0,4},{4,0},{8,12},{12,8},{1,5},{5,1},{9,13},{13,9},{2,6},{6,2},{1... | collective-permute-start | bytes 688136 | tf_op jit(solution)/shard_map/ppermute | solution.py:24
  16.8 16.0 %collective-permute-start.9 = (bf16[896,128]{1,0:T(8,128)(2,1)S(1)}, bf16[896,128]{1,0:T(8,128)(2,1)S(1)}, u32[]{:S(2)}, u32[]{:S(2)}) collective-permute-start(bf16[896,128]{1,0:T(8,128)(2,1)S(1)} %get-tuple-element.54), channel_id=1, source_target_pairs={{0,4},{4,0},{8,12},{12,8},{1,5},{5,1},{9,13},{13,9},{2,6},{6,2},{1... | collective-permute-start | bytes 688136 | tf_op jit(solution)/shard_map/ppermute | solution.py:24
  23.0 14.8 %collective-permute-start.4 = (bf16[896,128]{1,0:T(8,128)(2,1)S(1)}, bf16[896,128]{1,0:T(8,128)(2,1)S(1)}, u32[]{:S(2)}, u32[]{:S(2)}) collective-permute-start(bf16[896,128]{1,0:T(8,128)(2,1)S(1)} %get-tuple-element.48), channel_id=1, source_target_pairs={{0,4},{4,0},{8,12},{12,8},{1,5},{5,1},{9,13},{13,9},{2,6},{6,2},{1... | collective-permute-start | bytes 688136 | tf_op jit(solution)/shard_map/ppermute | solution.py:24
  24.9 12.9 %collective-permute-start.5 = (bf16[896,128]{1,0:T(8,128)(2,1)S(1)}, bf16[896,128]{1,0:T(8,128)(2,1)S(1)}, u32[]{:S(2)}, u32[]{:S(2)}) collective-permute-start(bf16[896,128]{1,0:T(8,128)(2,1)S(1)} %get-tuple-element.49), channel_id=1, source_target_pairs={{0,8},{4,12},{8,0},{12,4},{1,9},{5,13},{9,1},{13,5},{2,10},{6,14},... | collective-permute-start | bytes 688136 | tf_op jit(solution)/shard_map/ppermute | solution.py:24
  32.9 19.1 %collective-permute-start.10 = (bf16[896,128]{1,0:T(8,128)(2,1)S(1)}, bf16[896,128]{1,0:T(8,128)(2,1)S(1)}, u32[]{:S(2)}, u32[]{:S(2)}) collective-permute-start(bf16[896,128]{1,0:T(8,128)(2,1)S(1)} %get-tuple-element.56), channel_id=1, source_target_pairs={{0,4},{4,0},{8,12},{12,8},{1,5},{5,1},{9,13},{13,9},{2,6},{6,2},{1... | collective-permute-start | bytes 688136 | tf_op jit(solution)/shard_map/ppermute | solution.py:24
  32.9 19.0 %collective-permute-start.11 = (bf16[896,128]{1,0:T(8,128)(2,1)S(1)}, bf16[896,128]{1,0:T(8,128)(2,1)S(1)}, u32[]{:S(2)}, u32[]{:S(2)}) collective-permute-start(bf16[896,128]{1,0:T(8,128)(2,1)S(1)} %get-tuple-element.57), channel_id=1, source_target_pairs={{0,8},{4,12},{8,0},{12,4},{1,9},{5,13},{9,1},{13,5},{2,10},{6,14},... | collective-permute-start | bytes 688136 | tf_op jit(solution)/shard_map/ppermute | solution.py:24
  40.1 18.5 %collective-permute-start.7 = (bf16[896,128]{1,0:T(8,128)(2,1)S(1)}, bf16[896,128]{1,0:T(8,128)(2,1)S(1)}, u32[]{:S(2)}, u32[]{:S(2)}) collective-permute-start(bf16[896,128]{1,0:T(8,128)(2,1)S(1)} %get-tuple-element.50.rest_0_), channel_id=1, source_target_pairs={{0,4},{4,0},{8,12},{12,8},{1,5},{5,1},{9,13},{13,9},{2,6},{6,2},{1... | collective-permute-start | bytes 688136 | tf_op jit(solution)/shard_map/ppermute | solution.py:24
  42.9 18.2 %collective-permute-start.6 = (bf16[896,128]{1,0:T(8,128)(2,1)S(1)}, bf16[896,128]{1,0:T(8,128)(2,1)S(1)}, u32[]{:S(2)}, u32[]{:S(2)}) collective-permute-start(bf16[896,128]{1,0:T(8,128)(2,1)S(1)} %get-tuple-element.50.rest_0_), channel_id=1, source_target_pairs={{0,8},{4,12},{8,0},{12,4},{1,9},{5,13},{9,1},{13,5},{2,10},{6,14},... | collective-permute-start | bytes 688136 | tf_op jit(solution)/shard_map/ppermute | solution.py:24
  54.2 16.6 %collective-permute-start.14 = (bf16[896,128]{1,0:T(8,128)(2,1)S(1)}, bf16[896,128]{1,0:T(8,128)(2,1)S(1)}, u32[]{:S(2)}, u32[]{:S(2)}) collective-permute-start(bf16[896,128]{1,0:T(8,128)(2,1)S(1)} %get-tuple-element.61.rest_1_), channel_id=1, source_target_pairs={{0,4},{4,0},{8,12},{12,8},{1,5},{5,1},{9,13},{13,9},{2,6},{6,2},{1... | collective-permute-start | bytes 688136 | tf_op jit(solution)/shard_map/ppermute | solution.py:24
  54.2 12.5 %collective-permute-start.12 = (bf16[896,128]{1,0:T(8,128)(2,1)S(1)}, bf16[896,128]{1,0:T(8,128)(2,1)S(1)}, u32[]{:S(2)}, u32[]{:S(2)}) collective-permute-start(bf16[896,128]{1,0:T(8,128)(2,1)S(1)} %get-tuple-element.61.rest_1_), channel_id=1, source_target_pairs={{0,8},{4,12},{8,0},{12,4},{1,9},{5,13},{9,1},{13,5},{2,10},{6,14},... | collective-permute-start | bytes 688136 | tf_op jit(solution)/shard_map/ppermute | solution.py:24
  61.1 14.1 %collective-permute-start.8 = (bf16[896,128]{1,0:T(8,128)(2,1)S(1)}, bf16[896,128]{1,0:T(8,128)(2,1)S(1)}, u32[]{:S(2)}, u32[]{:S(2)}) collective-permute-start(bf16[896,128]{1,0:T(8,128)(2,1)S(1)} %pass_on.2), channel_id=1, source_target_pairs={{0,4},{4,0},{8,12},{12,8},{1,5},{5,1},{9,13},{13,9},{2,6},{6,2},{1... | collective-permute-start | bytes 688136 | tf_op jit(solution)/shard_map/ppermute | solution.py:24
  66.7 9.6 %collective-permute-start.13 = (bf16[896,128]{1,0:T(8,128)(2,1)S(1)}, bf16[896,128]{1,0:T(8,128)(2,1)S(1)}, u32[]{:S(2)}, u32[]{:S(2)}) collective-permute-start(bf16[896,128]{1,0:T(8,128)(2,1)S(1)} %pass_on.3), channel_id=1, source_target_pairs={{0,4},{4,0},{8,12},{12,8},{1,5},{5,1},{9,13},{13,9},{2,6},{6,2},{1... | collective-permute-start | bytes 688136 | tf_op jit(solution)/shard_map/ppermute | solution.py:24

commit v4 on v3

--- a/solution.py
+++ b/solution.py
@@ -260,6 +260,33 @@
     )(mine, other, activations, after)
 
 
+def bring(arrays, after):
+    count = len(arrays)
+
+    def kernel(*refs):
+        sems = refs[-1]
+        copies = [
+            pltpu.make_async_copy(refs[place], refs[count + 1 + place], sems.at[place])
+            for place in range(count)
+        ]
+        for copy in copies:
+            copy.start()
+        for copy in copies:
+            copy.wait()
+
+    return pl.pallas_call(
+        kernel,
+        in_specs=[pl.BlockSpec(memory_space=pltpu.HBM)] * count
+        + [pl.BlockSpec(memory_space=pl.ANY)],
+        out_specs=[pl.BlockSpec(memory_space=pltpu.VMEM)] * count,
+        out_shape=[jax.ShapeDtypeStruct(array.shape, array.dtype) for array in arrays],
+        scratch_shapes=[pltpu.SemaphoreType.DMA((count,))],
+        compiler_params=pltpu.CompilerParams(vmem_limit_bytes=VMEM),
+        cost_estimate=cost(0, 1000),
+        name="bring",
+    )(*arrays, after)
+
+
 def adam(own, near, far, first, second, chunk, before, after=()):
     rows, rank = far.shape
     tile = rows // 2
@@ -391,13 +418,15 @@
         token,
     )
     sum_a, near_a = merge(two_a, cross_a, near_a)
+    first_moment, second_moment, own = bring(
+        (fixed(first_moment), fixed(second_moment), fixed(own)), sum_a
+    )
     sum_a = swap(sum_a, "dp", 2)
     near_a = swap(near_a, "dp", 1)
     sum_b, near_b = merge(two_b, cross_b, near_b)
     sum_b = swap(sum_b, "dp", 2)
     near_b = swap(near_b, "dp", 1)
 
-    first_moment, second_moment, own = fixed(first_moment), fixed(second_moment), fixed(own)
     grow = functools.partial(expand, z[None], basis_cols, shape)
     rows_a, *moments = adam(own, near_a, sum_a, first_moment, second_moment, 0, None)
     far_a = swap(rows_a, "dp", 2)

time: 81 us -> 81 us (level)
    pallas_call x2, Pallas kernels: 4.54 us -> 2.23 us  [adam(): pl.pallas_call(kernel, grid=(2,), in_specs=[whole, local, local, whole, w...]
    pallas_call x0 -> x1, Pallas kernels: none -> 1.76 us  [bring(): pl.pallas_call(kernel, in_specs=[pl.BlockSpec(memory_space=pltpu.HBM)] *...]
  transfers between devices with their start and end apart: 15 -> 15, of which waited for: 8 -> 7; matrix products, arithmetic and copies ran while one was open for 0% -> 0% of each run, Pallas kernels for 33% -> 33%
where the time goes in v4:
time: 81 us; the launch traced here: 80.8 us
  Pallas kernels  33.5 us (41%)
  starting transfers between devices  32.4 us (40%)
  waiting for transfers between devices  14.1 us (17%)
    ppermute x15, starting transfers between devices, swap(): return lax.ppermute(value, axis, [(i, i ^ bit) for i in range(n)])  32.4 us
    pallas_call x5, Pallas kernels, expand(): pl.pallas_call(kernel, grid_spec=pltpu.PrefetchScalarGridSpec(num_scalar_...  18.5 us
    ppermute x15, waiting for transfers between devices, swap(): return lax.ppermute(value, axis, [(i, i ^ bit) for i in range(n)])  14.1 us
    pallas_call x1, Pallas kernels, low_rest(): pl.pallas_call(kernel, grid=(1,), in_specs=[pl.BlockSpec(memory_space=plt...  5.17 us
    pallas_call x1, Pallas kernels, project_give(): pl.pallas_call(kernel, in_specs=[pl.BlockSpec(memory_space=pltpu.HBM)] *...  2.23 us
    pallas_call x2, Pallas kernels, adam(): pl.pallas_call(kernel, grid=(2,), in_specs=[whole, local, local, whole, w...  2.23 us
    pallas_call x1, Pallas kernels, load(): pl.pallas_call(kernel, in_specs=[pl.BlockSpec(memory_space=pltpu.HBM)] *...  1.95 us
    pallas_call x1, Pallas kernels, bring(): pl.pallas_call(kernel, in_specs=[pl.BlockSpec(memory_space=pltpu.HBM)] *...  1.76 us
  transfers between devices with their start and end apart: 15, of which 7 were waited for; matrix products, arithmetic and copies ran while one was open for 0% of the time, Pallas kernels for 33%

profile of v4, /device:TPU:0, one launch (start us, length us, event | category | flops | bytes accessed | tf_op | source)
XLA Modules:
  0.0 80.8 jit_solution(5227314803610145278)
XLA Ops:
  0.6 2.2 %project_give.1 = (f32[128,384]{1,0:T(8,128)S(1)}, bf16[384,2048]{1,0:T(8,128)(2,1)S(1)}, bf16[2048,128]{1,0:T(8,128)(2,1)S(1)}) custom-call(bf16[768,2048]{1,0:T(8,128)(2,1)} %grad_hbm.1, bf16[8192,128]{1,0:T(8,128)(2,1)} %basis_hbm.3), custom_call_target="tpu_custom_call" | custom-call | flops 1000 | bytes 1000 | tf_op jit(solution)/shard_map/project_give/pallas_call | solution.py:62
  2.9 0.5 collective-permute-start
  3.4 0.6 project_keep.1.after_ref
  4.0 0.4 collective-permute-done
  4.5 2.9 %collective-permute-start.1 = (f32[128,384]{1,0:T(8,128)S(1)}, f32[128,384]{1,0:T(8,128)S(1)}, u32[]{:S(2)}, u32[]{:S(2)}) collective-permute-start(f32[128,384]{1,0:T(8,128)S(1)} %add.3.pair_ref), channel_id=1, source_target_pairs={{0,2},{1,3},{2,0},{3,1},{4,6},{5,7},{6,4},{7,5},{8,10},{9,11},{10,... | collective-permute-start | bytes 589832 | tf_op jit(solution)/shard_map/ppermute | solution.py:24
  7.4 2.0 %load.1 = (bf16[2,768,896]{2,1,0:T(8,128)(2,1)S(1)}, bf16[2048,128]{1,0:T(8,128)(2,1)S(1)}, f32[8,128]{1,0:T(8,128)S(1)}) custom-call(bf16[768,7168]{1,0:T(8,128)(2,1)} %act_hbm.3, bf16[8192,128]{1,0:T(8,128)(2,1)} %basis_hbm.3, f32[128,384]{1,0:T(8,128)S(1)} %project_keep.1.after_ref), custom_call_target="tpu_custom_call" | custom-call | bytes 2752512 | tf_op jit(solution)/shard_map/load/pallas_call | solution.py:182
  9.4 3.2 %collective-permute-done.1.far_ref = f32[128,384]{1,0:T(8,128)S(1)} collective-permute-done((f32[128,384]{1,0:T(8,128)S(1)}, f32[128,384]{1,0:T(8,128)S(1)}, u32[]{:S(2)}, u32[]{:S(2)}) %collective-permute-start.1) | collective-permute-done | bytes 196640 | tf_op jit(solution)/shard_map/ppermute | solution.py:24
  12.6 0.1 collective-permute-start.2
  12.7 1.3 %collective-permute-done.2.other_ref = bf16[128,384]{1,0:T(8,128)(2,1)S(1)} collective-permute-done((bf16[128,384]{1,0:T(8,128)(2,1)S(1)}, bf16[128,384]{1,0:T(8,128)(2,1)S(1)}, u32[]{:S(2)}, u32[]{:S(2)}) %collective-permute-start.2) | collective-permute-done | bytes 98336 | tf_op jit(solution)/shard_map/ppermute | solution.py:24
  14.0 0.5 low_held.2
  14.5 1.9 %collective-permute-start.3 = (bf16[896,128]{1,0:T(8,128)(2,1)S(1)}, bf16[896,128]{1,0:T(8,128)(2,1)S(1)}, u32[]{:S(2)}, u32[]{:S(2)}) collective-permute-start(bf16[896,128]{1,0:T(8,128)(2,1)S(1)} %get-tuple-element.49), channel_id=1, source_target_pairs={{0,4},{4,0},{8,12},{12,8},{1,5},{5,1},{9,13},{13,9},{2,6},{6,2},{1... | collective-permute-start | bytes 688136 | tf_op jit(solution)/shard_map/ppermute | solution.py:24
  16.4 0.4 low_held.3
  16.8 0.3 collective-permute-start.9
  17.1 5.2 %low_rest.1 = (f32[896,128]{1,0:T(8,128)S(1)}, bf16[896,128]{1,0:T(8,128)(2,1)S(1)}, f32[896,128]{1,0:T(8,128)S(1)}, bf16[896,128]{1,0:T(8,128)(2,1)S(1)}, f32[1792,128]{1,0:T(8,128)}) custom-call(bf16[128,384]{1,0:T(8,128)(2,1)S(1)} %settle.1.mine_ref, bf16[128,384]{1,0:T(8,128)(2,1)S(1)} %collective-permute-done.2.other_ref, bf16[768,7168]{1,0:T(8,128)(2,1)} %act_hbm.3, ...), custom_call_target="tpu_custom_call" | custom-call | flops 1000 | bytes 1000 | tf_op jit(solution)/shard_map/low_rest/pallas_call | solution.py:246
  22.3 0.7 collective-permute-done.3.got_ref
  23.0 0.1 merge.2
  23.0 1.9 %collective-permute-start.4 = (bf16[896,128]{1,0:T(8,128)(2,1)S(1)}, bf16[896,128]{1,0:T(8,128)(2,1)S(1)}, u32[]{:S(2)}, u32[]{:S(2)}) collective-permute-start(bf16[896,128]{1,0:T(8,128)(2,1)S(1)} %get-tuple-element.53), channel_id=1, source_target_pairs={{0,4},{4,0},{8,12},{12,8},{1,5},{5,1},{9,13},{13,9},{2,6},{6,2},{1... | collective-permute-start | bytes 688136 | tf_op jit(solution)/shard_map/ppermute | solution.py:24
  24.9 2.6 %collective-permute-start.5 = (bf16[896,128]{1,0:T(8,128)(2,1)S(1)}, bf16[896,128]{1,0:T(8,128)(2,1)S(1)}, u32[]{:S(2)}, u32[]{:S(2)}) collective-permute-start(bf16[896,128]{1,0:T(8,128)(2,1)S(1)} %get-tuple-element.51.refs_3_), channel_id=1, source_target_pairs={{0,8},{4,12},{8,0},{12,4},{1,9},{5,13},{9,1},{13,5},{2,10},{6,14},... | collective-permute-start | bytes 688136 | tf_op jit(solution)/shard_map/ppermute | solution.py:24
  27.5 5.3 %collective-permute-done.9.got_ref = bf16[896,128]{1,0:T(8,128)(2,1)S(1)} collective-permute-done((bf16[896,128]{1,0:T(8,128)(2,1)S(1)}, bf16[896,128]{1,0:T(8,128)(2,1)S(1)}, u32[]{:S(2)}, u32[]{:S(2)}) %collective-permute-start.9) | collective-permute-done | bytes 229408 | tf_op jit(solution)/shard_map/ppermute | solution.py:24
  32.9 0.1 collective-permute-start.10
  32.9 4.4 %collective-permute-start.11 = (bf16[896,128]{1,0:T(8,128)(2,1)S(1)}, bf16[896,128]{1,0:T(8,128)(2,1)S(1)}, u32[]{:S(2)}, u32[]{:S(2)}) collective-permute-start(bf16[896,128]{1,0:T(8,128)(2,1)S(1)} %get-tuple-element.63), channel_id=1, source_target_pairs={{0,8},{4,12},{8,0},{12,4},{1,9},{5,13},{9,1},{13,5},{2,10},{6,14},... | collective-permute-start | bytes 688136 | tf_op jit(solution)/shard_map/ppermute | solution.py:24
  37.3 1.8 %bring.1 = (f32[1792,128]{1,0:T(8,128)S(1)}, f32[1792,128]{1,0:T(8,128)S(1)}, f32[1792,128]{1,0:T(8,128)S(1)}) custom-call(f32[1792,128]{1,0:T(8,128)} %refs_0_.1, f32[1792,128]{1,0:T(8,128)} %refs_1_.1, f32[1792,128]{1,0:T(8,128)} %get-tuple-element.47.refs_2_, bf16[896,128]{1,0:T(8,128)(2,1)S(1)} %get-tuple-element.51.refs_3_), custom_call_target="tpu_custom_call" | custom-call | bytes 1000 | tf_op jit(solution)/shard_map/bring/pallas_call | solution.py:277
  39.1 0.0 collective-permute-done.4.near_ref
  39.1 0.0 collective-permute-done.5.far_ref
  39.1 1.1 %adam.2 = (bf16[896,128]{1,0:T(8,128)(2,1)S(1)}, f32[1792,128]{1,0:T(8,128)}, f32[1792,128]{1,0:T(8,128)}) custom-call(f32[1792,128]{1,0:T(8,128)S(1)} %get-tuple-element.52.own_ref, bf16[896,128]{1,0:T(8,128)(2,1)S(1)} %collective-permute-done.4.near_ref, bf16[896,128]{1,0:T(8,128)(2,1)S(1)} %collective-permute-done.5.far_ref, ...), custom_call_target="tpu_custom_call" | custom-call | flops 3440640 | bytes 2752512 | tf_op jit(solution)/shard_map/adam/pallas_call | solution.py:314
  40.3 1.5 %collective-permute-start.7 = (bf16[896,128]{1,0:T(8,128)(2,1)S(1)}, bf16[896,128]{1,0:T(8,128)(2,1)S(1)}, u32[]{:S(2)}, u32[]{:S(2)}) collective-permute-start(bf16[896,128]{1,0:T(8,128)(2,1)S(1)} %get-tuple-element.56.rest_0_), channel_id=1, source_target_pairs={{0,4},{4,0},{8,12},{12,8},{1,5},{5,1},{9,13},{13,9},{2,6},{6,2},{1... | collective-permute-start | bytes 688136 | tf_op jit(solution)/shard_map/ppermute | solution.py:24
  41.7 6.5 %collective-permute-start.6 = (bf16[896,128]{1,0:T(8,128)(2,1)S(1)}, bf16[896,128]{1,0:T(8,128)(2,1)S(1)}, u32[]{:S(2)}, u32[]{:S(2)}) collective-permute-start(bf16[896,128]{1,0:T(8,128)(2,1)S(1)} %get-tuple-element.56.rest_0_), channel_id=1, source_target_pairs={{0,8},{4,12},{8,0},{12,4},{1,9},{5,13},{9,1},{13,5},{2,10},{6,14},... | collective-permute-start | bytes 688136 | tf_op jit(solution)/shard_map/ppermute | solution.py:24
  48.2 2.5 %expand.5 = (bf16[7168,2048]{1,0:T(8,128)(2,1)}, f32[8,128]{1,0:T(8,128)S(1)}) custom-call(s32[1]{0:T(128)} %bitcast.s, bf16[2048,128]{1,0:T(8,128)(2,1)S(1)} %get-tuple-element.41.basis_ref, bf16[896,128]{1,0:T(8,128)(2,1)S(1)} %get-tuple-element.56.rest_0_), custom_call_target="tpu_custom_call" | custom-call | flops 14092861440 | bytes 110100480 | tf_op jit(solution)/shard_map/expand/pallas_call | solution.py:367
  50.8 0.0 collective-permute-done.10.near_ref
  50.8 0.0 collective-permute-done.11.far_ref
  50.8 1.1 %adam.3 = (bf16[896,128]{1,0:T(8,128)(2,1)S(1)}, f32[1792,128]{1,0:T(8,128)}, f32[1792,128]{1,0:T(8,128)}) custom-call(f32[1792,128]{1,0:T(8,128)S(1)} %get-tuple-element.52.own_ref, bf16[896,128]{1,0:T(8,128)(2,1)S(1)} %collective-permute-done.10.near_ref, ...), custom_call_target="tpu_custom_call", output_to_operand_aliasing={{1}: (5, {}), {2}: (6, {})} | custom-call | flops 3440640 | bytes 2752512 | tf_op jit(solution)/shard_map/adam/pallas_call | solution.py:314
  51.9 0.0 collective-permute-start.14
  51.9 6.2 %collective-permute-start.12 = (bf16[896,128]{1,0:T(8,128)(2,1)S(1)}, bf16[896,128]{1,0:T(8,128)(2,1)S(1)}, u32[]{:S(2)}, u32[]{:S(2)}) collective-permute-start(bf16[896,128]{1,0:T(8,128)(2,1)S(1)} %get-tuple-element.67.rest_1_), channel_id=1, source_target_pairs={{0,8},{4,12},{8,0},{12,4},{1,9},{5,13},{9,1},{13,5},{2,10},{6,14},... | collective-permute-start | bytes 688136 | tf_op jit(solution)/shard_map/ppermute | solution.py:24
  58.0 0.0 collective-permute-done.7.rest_0_
  58.0 2.6 %expand.6 = (bf16[7168,2048]{1,0:T(8,128)(2,1)}, f32[8,128]{1,0:T(8,128)S(1)}) custom-call(s32[1]{0:T(128)} %bitcast.s, bf16[2048,128]{1,0:T(8,128)(2,1)S(1)} %get-tuple-element.41.basis_ref, bf16[896,128]{1,0:T(8,128)(2,1)S(1)} %collective-permute-done.7.rest_0_, bf16[7168,2048]{1,0:T(8,128)(2,1)} %get-tuple-element.57.rest_1_), custom_call_target="tpu_custom_call", output_to_operand_aliasing={{0}: (3, {})} | custom-call | flops 14092861440 | bytes 110100480 | tf_op jit(solution)/shard_map/expand/pallas_call | solution.py:367
  60.6 0.0 collective-permute-done.6.value_ref.rest_0_
  60.6 0.1 collective-permute-start.8
  60.7 4.5 %expand.7 = (bf16[7168,2048]{1,0:T(8,128)(2,1)}, f32[8,128]{1,0:T(8,128)S(1)}) custom-call(s32[1]{0:T(128)} %bitcast.s, bf16[2048,128]{1,0:T(8,128)(2,1)S(1)} %get-tuple-element.41.basis_ref, bf16[896,128]{1,0:T(8,128)(2,1)S(1)} %collective-permute-done.6.value_ref.rest_0_, ...), custom_call_target="tpu_custom_call", output_to_operand_aliasing={{0}: (4, {})} | custom-call | flops 28185722880 | bytes 220200960 | tf_op jit(solution)/shard_map/expand/pallas_call | solution.py:367
  65.2 1.5 %collective-permute-done.12.value_ref.rest_1_ = bf16[896,128]{1,0:T(8,128)(2,1)S(1)} collective-permute-done((bf16[896,128]{1,0:T(8,128)(2,1)S(1)}, bf16[896,128]{1,0:T(8,128)(2,1)S(1)}, u32[]{:S(2)}, u32[]{:S(2)}) %collective-permute-start.12) | collective-permute-done | bytes 229408 | tf_op jit(solution)/shard_map/ppermute | solution.py:24
  66.7 3.6 %collective-permute-start.13 = (bf16[896,128]{1,0:T(8,128)(2,1)S(1)}, bf16[896,128]{1,0:T(8,128)(2,1)S(1)}, u32[]{:S(2)}, u32[]{:S(2)}) collective-permute-start(bf16[896,128]{1,0:T(8,128)(2,1)S(1)} %pass_on.3), channel_id=1, source_target_pairs={{0,4},{4,0},{8,12},{12,8},{1,5},{5,1},{9,13},{13,9},{2,6},{6,2},{1... | collective-permute-start | bytes 688136 | tf_op jit(solution)/shard_map/ppermute | solution.py:24
  70.3 0.0 collective-permute-done.14.rest_0_
  70.3 4.4 %expand.8 = (bf16[7168,2048]{1,0:T(8,128)(2,1)}, f32[8,128]{1,0:T(8,128)}) custom-call(s32[1]{0:T(128)} %bitcast.s, bf16[2048,128]{1,0:T(8,128)(2,1)S(1)} %get-tuple-element.41.basis_ref, bf16[896,128]{1,0:T(8,128)(2,1)S(1)} %collective-permute-done.14.rest_0_, ...), custom_call_target="tpu_custom_call", output_to_operand_aliasing={{0}: (4, {})} | custom-call | flops 28185722880 | bytes 220200960 | tf_op jit(solution)/shard_map/expand/pallas_call | solution.py:367
  74.7 0.0 collective-permute-done.8.rest_0_
  74.7 1.6 %collective-permute-done.13.rest_1_ = bf16[896,128]{1,0:T(8,128)(2,1)S(1)} collective-permute-done((bf16[896,128]{1,0:T(8,128)(2,1)S(1)}, bf16[896,128]{1,0:T(8,128)(2,1)S(1)}, u32[]{:S(2)}, u32[]{:S(2)}) %collective-permute-start.13) | collective-permute-done | bytes 229408 | tf_op jit(solution)/shard_map/ppermute | solution.py:24
  76.4 4.4 %expand.9 = (bf16[7168,2048]{1,0:T(8,128)(2,1)}, f32[8,128]{1,0:T(8,128)}) custom-call(s32[1]{0:T(128)} %bitcast.s, bf16[2048,128]{1,0:T(8,128)(2,1)S(1)} %get-tuple-element.41.basis_ref, bf16[896,128]{1,0:T(8,128)(2,1)S(1)} %collective-permute-done.8.rest_0_, bf16[896,128]{1,0:T(8,128)(2,1)S(1)} %collective-permute-done.13.rest_1_, ...), custom_call_target="tpu_custom_call", output_to_operand_aliasing={{0}: (4, {})} | custom-call | flops 28185722880 | bytes 220200960 | tf_op jit(solution)/shard_map/expand/pallas_call | solution.py:367
  (5 shorter events, 0.1 us)
Async XLA Ops:
  2.9 1.6 %collective-permute-start = (f32[128,384]{1,0:T(8,128)S(1)}, f32[128,384]{1,0:T(8,128)S(1)}, u32[]{:S(2)}, u32[]{:S(2)}) collective-permute-start(f32[128,384]{1,0:T(8,128)S(1)} %get-tuple-element.42), channel_id=1, source_target_pairs={{0,1},{1,0},{2,3},{3,2},{4,5},{5,4},{6,7},{7,6},{8,9},{9,8},{10,11... | collective-permute-start | bytes 589832 | tf_op jit(solution)/shard_map/ppermute | solution.py:24
  4.5 8.1 %collective-permute-start.1 = (f32[128,384]{1,0:T(8,128)S(1)}, f32[128,384]{1,0:T(8,128)S(1)}, u32[]{:S(2)}, u32[]{:S(2)}) collective-permute-start(f32[128,384]{1,0:T(8,128)S(1)} %add.3.pair_ref), channel_id=1, source_target_pairs={{0,2},{1,3},{2,0},{3,1},{4,6},{5,7},{6,4},{7,5},{8,10},{9,11},{10,... | collective-permute-start | bytes 589832 | tf_op jit(solution)/shard_map/ppermute | solution.py:24
  12.6 1.4 %collective-permute-start.2 = (bf16[128,384]{1,0:T(8,128)(2,1)S(1)}, bf16[128,384]{1,0:T(8,128)(2,1)S(1)}, u32[]{:S(2)}, u32[]{:S(2)}) collective-permute-start(bf16[128,384]{1,0:T(8,128)(2,1)S(1)} %settle.1.mine_ref), channel_id=1, source_target_pairs={{0,1},{1,0},{2,3},{3,2},{4,5},{5,4},{6,7},{7,6},{8,9},{9,8},{10,11... | collective-permute-start | bytes 294920 | tf_op jit(solution)/shard_map/ppermute | solution.py:24
  14.5 8.5 %collective-permute-start.3 = (bf16[896,128]{1,0:T(8,128)(2,1)S(1)}, bf16[896,128]{1,0:T(8,128)(2,1)S(1)}, u32[]{:S(2)}, u32[]{:S(2)}) collective-permute-start(bf16[896,128]{1,0:T(8,128)(2,1)S(1)} %get-tuple-element.49), channel_id=1, source_target_pairs={{0,4},{4,0},{8,12},{12,8},{1,5},{5,1},{9,13},{13,9},{2,6},{6,2},{1... | collective-permute-start | bytes 688136 | tf_op jit(solution)/shard_map/ppermute | solution.py:24
  16.8 16.0 %collective-permute-start.9 = (bf16[896,128]{1,0:T(8,128)(2,1)S(1)}, bf16[896,128]{1,0:T(8,128)(2,1)S(1)}, u32[]{:S(2)}, u32[]{:S(2)}) collective-permute-start(bf16[896,128]{1,0:T(8,128)(2,1)S(1)} %get-tuple-element.60), channel_id=1, source_target_pairs={{0,4},{4,0},{8,12},{12,8},{1,5},{5,1},{9,13},{13,9},{2,6},{6,2},{1... | collective-permute-start | bytes 688136 | tf_op jit(solution)/shard_map/ppermute | solution.py:24
  23.0 16.1 %collective-permute-start.4 = (bf16[896,128]{1,0:T(8,128)(2,1)S(1)}, bf16[896,128]{1,0:T(8,128)(2,1)S(1)}, u32[]{:S(2)}, u32[]{:S(2)}) collective-permute-start(bf16[896,128]{1,0:T(8,128)(2,1)S(1)} %get-tuple-element.53), channel_id=1, source_target_pairs={{0,4},{4,0},{8,12},{12,8},{1,5},{5,1},{9,13},{13,9},{2,6},{6,2},{1... | collective-permute-start | bytes 688136 | tf_op jit(solution)/shard_map/ppermute | solution.py:24
  24.9 14.2 %collective-permute-start.5 = (bf16[896,128]{1,0:T(8,128)(2,1)S(1)}, bf16[896,128]{1,0:T(8,128)(2,1)S(1)}, u32[]{:S(2)}, u32[]{:S(2)}) collective-permute-start(bf16[896,128]{1,0:T(8,128)(2,1)S(1)} %get-tuple-element.51.refs_3_), channel_id=1, source_target_pairs={{0,8},{4,12},{8,0},{12,4},{1,9},{5,13},{9,1},{13,5},{2,10},{6,14},... | collective-permute-start | bytes 688136 | tf_op jit(solution)/shard_map/ppermute | solution.py:24
  32.9 17.9 %collective-permute-start.10 = (bf16[896,128]{1,0:T(8,128)(2,1)S(1)}, bf16[896,128]{1,0:T(8,128)(2,1)S(1)}, u32[]{:S(2)}, u32[]{:S(2)}) collective-permute-start(bf16[896,128]{1,0:T(8,128)(2,1)S(1)} %get-tuple-element.62), channel_id=1, source_target_pairs={{0,4},{4,0},{8,12},{12,8},{1,5},{5,1},{9,13},{13,9},{2,6},{6,2},{1... | collective-permute-start | bytes 688136 | tf_op jit(solution)/shard_map/ppermute | solution.py:24
  32.9 17.8 %collective-permute-start.11 = (bf16[896,128]{1,0:T(8,128)(2,1)S(1)}, bf16[896,128]{1,0:T(8,128)(2,1)S(1)}, u32[]{:S(2)}, u32[]{:S(2)}) collective-permute-start(bf16[896,128]{1,0:T(8,128)(2,1)S(1)} %get-tuple-element.63), channel_id=1, source_target_pairs={{0,8},{4,12},{8,0},{12,4},{1,9},{5,13},{9,1},{13,5},{2,10},{6,14},... | collective-permute-start | bytes 688136 | tf_op jit(solution)/shard_map/ppermute | solution.py:24
  40.3 17.8 %collective-permute-start.7 = (bf16[896,128]{1,0:T(8,128)(2,1)S(1)}, bf16[896,128]{1,0:T(8,128)(2,1)S(1)}, u32[]{:S(2)}, u32[]{:S(2)}) collective-permute-start(bf16[896,128]{1,0:T(8,128)(2,1)S(1)} %get-tuple-element.56.rest_0_), channel_id=1, source_target_pairs={{0,4},{4,0},{8,12},{12,8},{1,5},{5,1},{9,13},{13,9},{2,6},{6,2},{1... | collective-permute-start | bytes 688136 | tf_op jit(solution)/shard_map/ppermute | solution.py:24
  41.7 18.9 %collective-permute-start.6 = (bf16[896,128]{1,0:T(8,128)(2,1)S(1)}, bf16[896,128]{1,0:T(8,128)(2,1)S(1)}, u32[]{:S(2)}, u32[]{:S(2)}) collective-permute-start(bf16[896,128]{1,0:T(8,128)(2,1)S(1)} %get-tuple-element.56.rest_0_), channel_id=1, source_target_pairs={{0,8},{4,12},{8,0},{12,4},{1,9},{5,13},{9,1},{13,5},{2,10},{6,14},... | collective-permute-start | bytes 688136 | tf_op jit(solution)/shard_map/ppermute | solution.py:24
  51.9 18.4 %collective-permute-start.14 = (bf16[896,128]{1,0:T(8,128)(2,1)S(1)}, bf16[896,128]{1,0:T(8,128)(2,1)S(1)}, u32[]{:S(2)}, u32[]{:S(2)}) collective-permute-start(bf16[896,128]{1,0:T(8,128)(2,1)S(1)} %get-tuple-element.67.rest_1_), channel_id=1, source_target_pairs={{0,4},{4,0},{8,12},{12,8},{1,5},{5,1},{9,13},{13,9},{2,6},{6,2},{1... | collective-permute-start | bytes 688136 | tf_op jit(solution)/shard_map/ppermute | solution.py:24
  51.9 14.8 %collective-permute-start.12 = (bf16[896,128]{1,0:T(8,128)(2,1)S(1)}, bf16[896,128]{1,0:T(8,128)(2,1)S(1)}, u32[]{:S(2)}, u32[]{:S(2)}) collective-permute-start(bf16[896,128]{1,0:T(8,128)(2,1)S(1)} %get-tuple-element.67.rest_1_), channel_id=1, source_target_pairs={{0,8},{4,12},{8,0},{12,4},{1,9},{5,13},{9,1},{13,5},{2,10},{6,14},... | collective-permute-start | bytes 688136 | tf_op jit(solution)/shard_map/ppermute | solution.py:24
  60.6 14.1 %collective-permute-start.8 = (bf16[896,128]{1,0:T(8,128)(2,1)S(1)}, bf16[896,128]{1,0:T(8,128)(2,1)S(1)}, u32[]{:S(2)}, u32[]{:S(2)}) collective-permute-start(bf16[896,128]{1,0:T(8,128)(2,1)S(1)} %pass_on.2), channel_id=1, source_target_pairs={{0,4},{4,0},{8,12},{12,8},{1,5},{5,1},{9,13},{13,9},{2,6},{6,2},{1... | collective-permute-start | bytes 688136 | tf_op jit(solution)/shard_map/ppermute | solution.py:24
  66.7 9.7 %collective-permute-start.13 = (bf16[896,128]{1,0:T(8,128)(2,1)S(1)}, bf16[896,128]{1,0:T(8,128)(2,1)S(1)}, u32[]{:S(2)}, u32[]{:S(2)}) collective-permute-start(bf16[896,128]{1,0:T(8,128)(2,1)S(1)} %pass_on.3), channel_id=1, source_target_pairs={{0,4},{4,0},{8,12},{12,8},{1,5},{5,1},{9,13},{13,9},{2,6},{6,2},{1... | collective-permute-start | bytes 688136 | tf_op jit(solution)/shard_map/ppermute | solution.py:24

commit v5 on v4

--- a/solution.py
+++ b/solution.py
@@ -289,7 +289,7 @@
 
 def adam(own, near, far, first, second, chunk, before, after=()):
     rows, rank = far.shape
-    tile = rows // 2
+    tile = rows
     first_fix = 1.0 - 0.9**STEP
     second_fix = 1.0 - 0.999**STEP
 
@@ -309,11 +309,11 @@
         ).astype(jnp.bfloat16)
 
     local = pl.BlockSpec((tile, rank), lambda i: (i, 0))
-    whole = pl.BlockSpec((tile, rank), lambda i: (chunk * 2 + i, 0))
+    whole = pl.BlockSpec((tile, rank), lambda i: (chunk + i, 0))
     extra = [] if before is None else list(before)
     return pl.pallas_call(
         kernel,
-        grid=(2,),
+        grid=(1,),
         in_specs=[whole, local, local, whole, whole]
         + [pl.BlockSpec(memory_space=pl.ANY)] * (len(extra) + len(after)),
         out_specs=[local, whole, whole],

time: 81 us -> 81 us (level)
  no operation moved by 1% of the time
where the time goes in v5:
time: 81 us; the launch traced here: 80.8 us
  Pallas kernels  33.6 us (41%)
  starting transfers between devices  32.4 us (40%)
  waiting for transfers between devices  14 us (17%)
    ppermute x15, starting transfers between devices, swap(): return lax.ppermute(value, axis, [(i, i ^ bit) for i in range(n)])  32.4 us
    pallas_call x5, Pallas kernels, expand(): pl.pallas_call(kernel, grid_spec=pltpu.PrefetchScalarGridSpec(num_scalar_...  18.5 us
    ppermute x15, waiting for transfers between devices, swap(): return lax.ppermute(value, axis, [(i, i ^ bit) for i in range(n)])  14 us
    pallas_call x1, Pallas kernels, low_rest(): pl.pallas_call(kernel, grid=(1,), in_specs=[pl.BlockSpec(memory_space=plt...  5.17 us
    pallas_call x2, Pallas kernels, adam(): pl.pallas_call(kernel, grid=(1,), in_specs=[whole, local, local, whole, w...  2.3 us
    pallas_call x1, Pallas kernels, project_give(): pl.pallas_call(kernel, in_specs=[pl.BlockSpec(memory_space=pltpu.HBM)] *...  2.23 us
    pallas_call x1, Pallas kernels, load(): pl.pallas_call(kernel, in_specs=[pl.BlockSpec(memory_space=pltpu.HBM)] *...  1.95 us
    pallas_call x1, Pallas kernels, bring(): pl.pallas_call(kernel, in_specs=[pl.BlockSpec(memory_space=pltpu.HBM)] *...  1.76 us
  transfers between devices with their start and end apart: 15, of which 7 were waited for; matrix products, arithmetic and copies ran while one was open for 0% of the time, Pallas kernels for 33%

profile of v5, /device:TPU:0, one launch (start us, length us, event | category | flops | bytes accessed | tf_op | source)
XLA Modules:
  0.0 80.8 jit_solution(16150326794706470315)
XLA Ops:
  0.6 2.2 %project_give.1 = (f32[128,384]{1,0:T(8,128)S(1)}, bf16[384,2048]{1,0:T(8,128)(2,1)S(1)}, bf16[2048,128]{1,0:T(8,128)(2,1)S(1)}) custom-call(bf16[768,2048]{1,0:T(8,128)(2,1)} %grad_hbm.1, bf16[8192,128]{1,0:T(8,128)(2,1)} %basis_hbm.3), custom_call_target="tpu_custom_call" | custom-call | flops 1000 | bytes 1000 | tf_op jit(solution)/shard_map/project_give/pallas_call | solution.py:62
  2.9 0.5 collective-permute-start
  3.4 0.6 project_keep.1.after_ref
  4.0 0.4 collective-permute-done
  4.5 2.9 %collective-permute-start.1 = (f32[128,384]{1,0:T(8,128)S(1)}, f32[128,384]{1,0:T(8,128)S(1)}, u32[]{:S(2)}, u32[]{:S(2)}) collective-permute-start(f32[128,384]{1,0:T(8,128)S(1)} %add.3.pair_ref), channel_id=1, source_target_pairs={{0,2},{1,3},{2,0},{3,1},{4,6},{5,7},{6,4},{7,5},{8,10},{9,11},{10,... | collective-permute-start | bytes 589832 | tf_op jit(solution)/shard_map/ppermute | solution.py:24
  7.4 2.0 %load.1 = (bf16[2,768,896]{2,1,0:T(8,128)(2,1)S(1)}, bf16[2048,128]{1,0:T(8,128)(2,1)S(1)}, f32[8,128]{1,0:T(8,128)S(1)}) custom-call(bf16[768,7168]{1,0:T(8,128)(2,1)} %act_hbm.3, bf16[8192,128]{1,0:T(8,128)(2,1)} %basis_hbm.3, f32[128,384]{1,0:T(8,128)S(1)} %project_keep.1.after_ref), custom_call_target="tpu_custom_call" | custom-call | bytes 2752512 | tf_op jit(solution)/shard_map/load/pallas_call | solution.py:182
  9.4 3.2 %collective-permute-done.1.far_ref = f32[128,384]{1,0:T(8,128)S(1)} collective-permute-done((f32[128,384]{1,0:T(8,128)S(1)}, f32[128,384]{1,0:T(8,128)S(1)}, u32[]{:S(2)}, u32[]{:S(2)}) %collective-permute-start.1) | collective-permute-done | bytes 196640 | tf_op jit(solution)/shard_map/ppermute | solution.py:24
  12.6 0.1 collective-permute-start.2
  12.7 1.3 %collective-permute-done.2.other_ref = bf16[128,384]{1,0:T(8,128)(2,1)S(1)} collective-permute-done((bf16[128,384]{1,0:T(8,128)(2,1)S(1)}, bf16[128,384]{1,0:T(8,128)(2,1)S(1)}, u32[]{:S(2)}, u32[]{:S(2)}) %collective-permute-start.2) | collective-permute-done | bytes 98336 | tf_op jit(solution)/shard_map/ppermute | solution.py:24
  14.0 0.5 low_held.2
  14.5 1.9 %collective-permute-start.3 = (bf16[896,128]{1,0:T(8,128)(2,1)S(1)}, bf16[896,128]{1,0:T(8,128)(2,1)S(1)}, u32[]{:S(2)}, u32[]{:S(2)}) collective-permute-start(bf16[896,128]{1,0:T(8,128)(2,1)S(1)} %get-tuple-element.49), channel_id=1, source_target_pairs={{0,4},{4,0},{8,12},{12,8},{1,5},{5,1},{9,13},{13,9},{2,6},{6,2},{1... | collective-permute-start | bytes 688136 | tf_op jit(solution)/shard_map/ppermute | solution.py:24
  16.4 0.4 low_held.3
  16.8 0.3 collective-permute-start.9
  17.1 5.2 %low_rest.1 = (f32[896,128]{1,0:T(8,128)S(1)}, bf16[896,128]{1,0:T(8,128)(2,1)S(1)}, f32[896,128]{1,0:T(8,128)S(1)}, bf16[896,128]{1,0:T(8,128)(2,1)S(1)}, f32[1792,128]{1,0:T(8,128)}) custom-call(bf16[128,384]{1,0:T(8,128)(2,1)S(1)} %settle.1.mine_ref, bf16[128,384]{1,0:T(8,128)(2,1)S(1)} %collective-permute-done.2.other_ref, bf16[768,7168]{1,0:T(8,128)(2,1)} %act_hbm.3, ...), custom_call_target="tpu_custom_call" | custom-call | flops 1000 | bytes 1000 | tf_op jit(solution)/shard_map/low_rest/pallas_call | solution.py:246
  22.3 0.7 collective-permute-done.3.got_ref
  23.0 0.1 merge.2
  23.0 1.9 %collective-permute-start.4 = (bf16[896,128]{1,0:T(8,128)(2,1)S(1)}, bf16[896,128]{1,0:T(8,128)(2,1)S(1)}, u32[]{:S(2)}, u32[]{:S(2)}) collective-permute-start(bf16[896,128]{1,0:T(8,128)(2,1)S(1)} %get-tuple-element.53), channel_id=1, source_target_pairs={{0,4},{4,0},{8,12},{12,8},{1,5},{5,1},{9,13},{13,9},{2,6},{6,2},{1... | collective-permute-start | bytes 688136 | tf_op jit(solution)/shard_map/ppermute | solution.py:24
  24.9 2.6 %collective-permute-start.5 = (bf16[896,128]{1,0:T(8,128)(2,1)S(1)}, bf16[896,128]{1,0:T(8,128)(2,1)S(1)}, u32[]{:S(2)}, u32[]{:S(2)}) collective-permute-start(bf16[896,128]{1,0:T(8,128)(2,1)S(1)} %get-tuple-element.51.refs_3_), channel_id=1, source_target_pairs={{0,8},{4,12},{8,0},{12,4},{1,9},{5,13},{9,1},{13,5},{2,10},{6,14},... | collective-permute-start | bytes 688136 | tf_op jit(solution)/shard_map/ppermute | solution.py:24
  27.5 5.3 %collective-permute-done.9.got_ref = bf16[896,128]{1,0:T(8,128)(2,1)S(1)} collective-permute-done((bf16[896,128]{1,0:T(8,128)(2,1)S(1)}, bf16[896,128]{1,0:T(8,128)(2,1)S(1)}, u32[]{:S(2)}, u32[]{:S(2)}) %collective-permute-start.9) | collective-permute-done | bytes 229408 | tf_op jit(solution)/shard_map/ppermute | solution.py:24
  32.9 0.1 collective-permute-start.10
  32.9 4.4 %collective-permute-start.11 = (bf16[896,128]{1,0:T(8,128)(2,1)S(1)}, bf16[896,128]{1,0:T(8,128)(2,1)S(1)}, u32[]{:S(2)}, u32[]{:S(2)}) collective-permute-start(bf16[896,128]{1,0:T(8,128)(2,1)S(1)} %get-tuple-element.63), channel_id=1, source_target_pairs={{0,8},{4,12},{8,0},{12,4},{1,9},{5,13},{9,1},{13,5},{2,10},{6,14},... | collective-permute-start | bytes 688136 | tf_op jit(solution)/shard_map/ppermute | solution.py:24
  37.3 1.8 %bring.1 = (f32[1792,128]{1,0:T(8,128)S(1)}, f32[1792,128]{1,0:T(8,128)S(1)}, f32[1792,128]{1,0:T(8,128)S(1)}) custom-call(f32[1792,128]{1,0:T(8,128)} %refs_0_.1, f32[1792,128]{1,0:T(8,128)} %refs_1_.1, f32[1792,128]{1,0:T(8,128)} %get-tuple-element.47.refs_2_, bf16[896,128]{1,0:T(8,128)(2,1)S(1)} %get-tuple-element.51.refs_3_), custom_call_target="tpu_custom_call" | custom-call | bytes 1000 | tf_op jit(solution)/shard_map/bring/pallas_call | solution.py:277
  39.1 0.0 collective-permute-done.4.near_ref
  39.1 0.0 collective-permute-done.5.far_ref
  39.1 1.2 %adam.2 = (bf16[896,128]{1,0:T(8,128)(2,1)S(1)}, f32[1792,128]{1,0:T(8,128)}, f32[1792,128]{1,0:T(8,128)}) custom-call(f32[1792,128]{1,0:T(8,128)S(1)} %get-tuple-element.52.own_ref, bf16[896,128]{1,0:T(8,128)(2,1)S(1)} %collective-permute-done.4.near_ref, bf16[896,128]{1,0:T(8,128)(2,1)S(1)} %collective-permute-done.5.far_ref, ...), custom_call_target="tpu_custom_call" | custom-call | flops 3440640 | bytes 2752512 | tf_op jit(solution)/shard_map/adam/pallas_call | solution.py:314
  40.3 1.5 %collective-permute-start.7 = (bf16[896,128]{1,0:T(8,128)(2,1)S(1)}, bf16[896,128]{1,0:T(8,128)(2,1)S(1)}, u32[]{:S(2)}, u32[]{:S(2)}) collective-permute-start(bf16[896,128]{1,0:T(8,128)(2,1)S(1)} %get-tuple-element.56.rest_0_), channel_id=1, source_target_pairs={{0,4},{4,0},{8,12},{12,8},{1,5},{5,1},{9,13},{13,9},{2,6},{6,2},{1... | collective-permute-start | bytes 688136 | tf_op jit(solution)/shard_map/ppermute | solution.py:24
  41.8 6.5 %collective-permute-start.6 = (bf16[896,128]{1,0:T(8,128)(2,1)S(1)}, bf16[896,128]{1,0:T(8,128)(2,1)S(1)}, u32[]{:S(2)}, u32[]{:S(2)}) collective-permute-start(bf16[896,128]{1,0:T(8,128)(2,1)S(1)} %get-tuple-element.56.rest_0_), channel_id=1, source_target_pairs={{0,8},{4,12},{8,0},{12,4},{1,9},{5,13},{9,1},{13,5},{2,10},{6,14},... | collective-permute-start | bytes 688136 | tf_op jit(solution)/shard_map/ppermute | solution.py:24
  48.3 2.5 %expand.5 = (bf16[7168,2048]{1,0:T(8,128)(2,1)}, f32[8,128]{1,0:T(8,128)S(1)}) custom-call(s32[1]{0:T(128)} %bitcast.s, bf16[2048,128]{1,0:T(8,128)(2,1)S(1)} %get-tuple-element.41.basis_ref, bf16[896,128]{1,0:T(8,128)(2,1)S(1)} %get-tuple-element.56.rest_0_), custom_call_target="tpu_custom_call" | custom-call | flops 14092861440 | bytes 110100480 | tf_op jit(solution)/shard_map/expand/pallas_call | solution.py:367
  50.8 0.0 collective-permute-done.10.near_ref
  50.8 0.0 collective-permute-done.11.far_ref
  50.8 1.1 %adam.3 = (bf16[896,128]{1,0:T(8,128)(2,1)S(1)}, f32[1792,128]{1,0:T(8,128)}, f32[1792,128]{1,0:T(8,128)}) custom-call(f32[1792,128]{1,0:T(8,128)S(1)} %get-tuple-element.52.own_ref, bf16[896,128]{1,0:T(8,128)(2,1)S(1)} %collective-permute-done.10.near_ref, ...), custom_call_target="tpu_custom_call", output_to_operand_aliasing={{1}: (5, {}), {2}: (6, {})} | custom-call | flops 3440640 | bytes 2752512 | tf_op jit(solution)/shard_map/adam/pallas_call | solution.py:314
  52.0 0.0 collective-permute-start.14
  52.0 6.1 %collective-permute-start.12 = (bf16[896,128]{1,0:T(8,128)(2,1)S(1)}, bf16[896,128]{1,0:T(8,128)(2,1)S(1)}, u32[]{:S(2)}, u32[]{:S(2)}) collective-permute-start(bf16[896,128]{1,0:T(8,128)(2,1)S(1)} %get-tuple-element.67.rest_1_), channel_id=1, source_target_pairs={{0,8},{4,12},{8,0},{12,4},{1,9},{5,13},{9,1},{13,5},{2,10},{6,14},... | collective-permute-start | bytes 688136 | tf_op jit(solution)/shard_map/ppermute | solution.py:24
  58.1 0.0 collective-permute-done.7.rest_0_
  58.1 2.6 %expand.6 = (bf16[7168,2048]{1,0:T(8,128)(2,1)}, f32[8,128]{1,0:T(8,128)S(1)}) custom-call(s32[1]{0:T(128)} %bitcast.s, bf16[2048,128]{1,0:T(8,128)(2,1)S(1)} %get-tuple-element.41.basis_ref, bf16[896,128]{1,0:T(8,128)(2,1)S(1)} %collective-permute-done.7.rest_0_, bf16[7168,2048]{1,0:T(8,128)(2,1)} %get-tuple-element.57.rest_1_), custom_call_target="tpu_custom_call", output_to_operand_aliasing={{0}: (3, {})} | custom-call | flops 14092861440 | bytes 110100480 | tf_op jit(solution)/shard_map/expand/pallas_call | solution.py:367
  60.7 0.0 collective-permute-done.6.value_ref.rest_0_
  60.7 0.1 collective-permute-start.8
  60.8 4.5 %expand.7 = (bf16[7168,2048]{1,0:T(8,128)(2,1)}, f32[8,128]{1,0:T(8,128)S(1)}) custom-call(s32[1]{0:T(128)} %bitcast.s, bf16[2048,128]{1,0:T(8,128)(2,1)S(1)} %get-tuple-element.41.basis_ref, bf16[896,128]{1,0:T(8,128)(2,1)S(1)} %collective-permute-done.6.value_ref.rest_0_, ...), custom_call_target="tpu_custom_call", output_to_operand_aliasing={{0}: (4, {})} | custom-call | flops 28185722880 | bytes 220200960 | tf_op jit(solution)/shard_map/expand/pallas_call | solution.py:367
  65.2 1.4 %collective-permute-done.12.value_ref.rest_1_ = bf16[896,128]{1,0:T(8,128)(2,1)S(1)} collective-permute-done((bf16[896,128]{1,0:T(8,128)(2,1)S(1)}, bf16[896,128]{1,0:T(8,128)(2,1)S(1)}, u32[]{:S(2)}, u32[]{:S(2)}) %collective-permute-start.12) | collective-permute-done | bytes 229408 | tf_op jit(solution)/shard_map/ppermute | solution.py:24
  66.7 3.6 %collective-permute-start.13 = (bf16[896,128]{1,0:T(8,128)(2,1)S(1)}, bf16[896,128]{1,0:T(8,128)(2,1)S(1)}, u32[]{:S(2)}, u32[]{:S(2)}) collective-permute-start(bf16[896,128]{1,0:T(8,128)(2,1)S(1)} %pass_on.3), channel_id=1, source_target_pairs={{0,4},{4,0},{8,12},{12,8},{1,5},{5,1},{9,13},{13,9},{2,6},{6,2},{1... | collective-permute-start | bytes 688136 | tf_op jit(solution)/shard_map/ppermute | solution.py:24
  70.3 0.0 collective-permute-done.14.rest_0_
  70.3 4.4 %expand.8 = (bf16[7168,2048]{1,0:T(8,128)(2,1)}, f32[8,128]{1,0:T(8,128)}) custom-call(s32[1]{0:T(128)} %bitcast.s, bf16[2048,128]{1,0:T(8,128)(2,1)S(1)} %get-tuple-element.41.basis_ref, bf16[896,128]{1,0:T(8,128)(2,1)S(1)} %collective-permute-done.14.rest_0_, ...), custom_call_target="tpu_custom_call", output_to_operand_aliasing={{0}: (4, {})} | custom-call | flops 28185722880 | bytes 220200960 | tf_op jit(solution)/shard_map/expand/pallas_call | solution.py:367
  74.7 0.0 collective-permute-done.8.rest_0_
  74.7 1.6 %collective-permute-done.13.rest_1_ = bf16[896,128]{1,0:T(8,128)(2,1)S(1)} collective-permute-done((bf16[896,128]{1,0:T(8,128)(2,1)S(1)}, bf16[896,128]{1,0:T(8,128)(2,1)S(1)}, u32[]{:S(2)}, u32[]{:S(2)}) %collective-permute-start.13) | collective-permute-done | bytes 229408 | tf_op jit(solution)/shard_map/ppermute | solution.py:24
  76.4 4.4 %expand.9 = (bf16[7168,2048]{1,0:T(8,128)(2,1)}, f32[8,128]{1,0:T(8,128)}) custom-call(s32[1]{0:T(128)} %bitcast.s, bf16[2048,128]{1,0:T(8,128)(2,1)S(1)} %get-tuple-element.41.basis_ref, bf16[896,128]{1,0:T(8,128)(2,1)S(1)} %collective-permute-done.8.rest_0_, bf16[896,128]{1,0:T(8,128)(2,1)S(1)} %collective-permute-done.13.rest_1_, ...), custom_call_target="tpu_custom_call", output_to_operand_aliasing={{0}: (4, {})} | custom-call | flops 28185722880 | bytes 220200960 | tf_op jit(solution)/shard_map/expand/pallas_call | solution.py:367
  (5 shorter events, 0.1 us)
Async XLA Ops:
  2.9 1.6 %collective-permute-start = (f32[128,384]{1,0:T(8,128)S(1)}, f32[128,384]{1,0:T(8,128)S(1)}, u32[]{:S(2)}, u32[]{:S(2)}) collective-permute-start(f32[128,384]{1,0:T(8,128)S(1)} %get-tuple-element.42), channel_id=1, source_target_pairs={{0,1},{1,0},{2,3},{3,2},{4,5},{5,4},{6,7},{7,6},{8,9},{9,8},{10,11... | collective-permute-start | bytes 589832 | tf_op jit(solution)/shard_map/ppermute | solution.py:24
  4.5 8.1 %collective-permute-start.1 = (f32[128,384]{1,0:T(8,128)S(1)}, f32[128,384]{1,0:T(8,128)S(1)}, u32[]{:S(2)}, u32[]{:S(2)}) collective-permute-start(f32[128,384]{1,0:T(8,128)S(1)} %add.3.pair_ref), channel_id=1, source_target_pairs={{0,2},{1,3},{2,0},{3,1},{4,6},{5,7},{6,4},{7,5},{8,10},{9,11},{10,... | collective-permute-start | bytes 589832 | tf_op jit(solution)/shard_map/ppermute | solution.py:24
  12.6 1.4 %collective-permute-start.2 = (bf16[128,384]{1,0:T(8,128)(2,1)S(1)}, bf16[128,384]{1,0:T(8,128)(2,1)S(1)}, u32[]{:S(2)}, u32[]{:S(2)}) collective-permute-start(bf16[128,384]{1,0:T(8,128)(2,1)S(1)} %settle.1.mine_ref), channel_id=1, source_target_pairs={{0,1},{1,0},{2,3},{3,2},{4,5},{5,4},{6,7},{7,6},{8,9},{9,8},{10,11... | collective-permute-start | bytes 294920 | tf_op jit(solution)/shard_map/ppermute | solution.py:24
  14.5 8.5 %collective-permute-start.3 = (bf16[896,128]{1,0:T(8,128)(2,1)S(1)}, bf16[896,128]{1,0:T(8,128)(2,1)S(1)}, u32[]{:S(2)}, u32[]{:S(2)}) collective-permute-start(bf16[896,128]{1,0:T(8,128)(2,1)S(1)} %get-tuple-element.49), channel_id=1, source_target_pairs={{0,4},{4,0},{8,12},{12,8},{1,5},{5,1},{9,13},{13,9},{2,6},{6,2},{1... | collective-permute-start | bytes 688136 | tf_op jit(solution)/shard_map/ppermute | solution.py:24
  16.8 16.0 %collective-permute-start.9 = (bf16[896,128]{1,0:T(8,128)(2,1)S(1)}, bf16[896,128]{1,0:T(8,128)(2,1)S(1)}, u32[]{:S(2)}, u32[]{:S(2)}) collective-permute-start(bf16[896,128]{1,0:T(8,128)(2,1)S(1)} %get-tuple-element.60), channel_id=1, source_target_pairs={{0,4},{4,0},{8,12},{12,8},{1,5},{5,1},{9,13},{13,9},{2,6},{6,2},{1... | collective-permute-start | bytes 688136 | tf_op jit(solution)/shard_map/ppermute | solution.py:24
  23.0 16.1 %collective-permute-start.4 = (bf16[896,128]{1,0:T(8,128)(2,1)S(1)}, bf16[896,128]{1,0:T(8,128)(2,1)S(1)}, u32[]{:S(2)}, u32[]{:S(2)}) collective-permute-start(bf16[896,128]{1,0:T(8,128)(2,1)S(1)} %get-tuple-element.53), channel_id=1, source_target_pairs={{0,4},{4,0},{8,12},{12,8},{1,5},{5,1},{9,13},{13,9},{2,6},{6,2},{1... | collective-permute-start | bytes 688136 | tf_op jit(solution)/shard_map/ppermute | solution.py:24
  24.9 14.2 %collective-permute-start.5 = (bf16[896,128]{1,0:T(8,128)(2,1)S(1)}, bf16[896,128]{1,0:T(8,128)(2,1)S(1)}, u32[]{:S(2)}, u32[]{:S(2)}) collective-permute-start(bf16[896,128]{1,0:T(8,128)(2,1)S(1)} %get-tuple-element.51.refs_3_), channel_id=1, source_target_pairs={{0,8},{4,12},{8,0},{12,4},{1,9},{5,13},{9,1},{13,5},{2,10},{6,14},... | collective-permute-start | bytes 688136 | tf_op jit(solution)/shard_map/ppermute | solution.py:24
  32.9 18.0 %collective-permute-start.10 = (bf16[896,128]{1,0:T(8,128)(2,1)S(1)}, bf16[896,128]{1,0:T(8,128)(2,1)S(1)}, u32[]{:S(2)}, u32[]{:S(2)}) collective-permute-start(bf16[896,128]{1,0:T(8,128)(2,1)S(1)} %get-tuple-element.62), channel_id=1, source_target_pairs={{0,4},{4,0},{8,12},{12,8},{1,5},{5,1},{9,13},{13,9},{2,6},{6,2},{1... | collective-permute-start | bytes 688136 | tf_op jit(solution)/shard_map/ppermute | solution.py:24
  32.9 17.9 %collective-permute-start.11 = (bf16[896,128]{1,0:T(8,128)(2,1)S(1)}, bf16[896,128]{1,0:T(8,128)(2,1)S(1)}, u32[]{:S(2)}, u32[]{:S(2)}) collective-permute-start(bf16[896,128]{1,0:T(8,128)(2,1)S(1)} %get-tuple-element.63), channel_id=1, source_target_pairs={{0,8},{4,12},{8,0},{12,4},{1,9},{5,13},{9,1},{13,5},{2,10},{6,14},... | collective-permute-start | bytes 688136 | tf_op jit(solution)/shard_map/ppermute | solution.py:24
  40.3 17.8 %collective-permute-start.7 = (bf16[896,128]{1,0:T(8,128)(2,1)S(1)}, bf16[896,128]{1,0:T(8,128)(2,1)S(1)}, u32[]{:S(2)}, u32[]{:S(2)}) collective-permute-start(bf16[896,128]{1,0:T(8,128)(2,1)S(1)} %get-tuple-element.56.rest_0_), channel_id=1, source_target_pairs={{0,4},{4,0},{8,12},{12,8},{1,5},{5,1},{9,13},{13,9},{2,6},{6,2},{1... | collective-permute-start | bytes 688136 | tf_op jit(solution)/shard_map/ppermute | solution.py:24
  41.8 18.9 %collective-permute-start.6 = (bf16[896,128]{1,0:T(8,128)(2,1)S(1)}, bf16[896,128]{1,0:T(8,128)(2,1)S(1)}, u32[]{:S(2)}, u32[]{:S(2)}) collective-permute-start(bf16[896,128]{1,0:T(8,128)(2,1)S(1)} %get-tuple-element.56.rest_0_), channel_id=1, source_target_pairs={{0,8},{4,12},{8,0},{12,4},{1,9},{5,13},{9,1},{13,5},{2,10},{6,14},... | collective-permute-start | bytes 688136 | tf_op jit(solution)/shard_map/ppermute | solution.py:24
  52.0 18.3 %collective-permute-start.14 = (bf16[896,128]{1,0:T(8,128)(2,1)S(1)}, bf16[896,128]{1,0:T(8,128)(2,1)S(1)}, u32[]{:S(2)}, u32[]{:S(2)}) collective-permute-start(bf16[896,128]{1,0:T(8,128)(2,1)S(1)} %get-tuple-element.67.rest_1_), channel_id=1, source_target_pairs={{0,4},{4,0},{8,12},{12,8},{1,5},{5,1},{9,13},{13,9},{2,6},{6,2},{1... | collective-permute-start | bytes 688136 | tf_op jit(solution)/shard_map/ppermute | solution.py:24
  52.0 14.7 %collective-permute-start.12 = (bf16[896,128]{1,0:T(8,128)(2,1)S(1)}, bf16[896,128]{1,0:T(8,128)(2,1)S(1)}, u32[]{:S(2)}, u32[]{:S(2)}) collective-permute-start(bf16[896,128]{1,0:T(8,128)(2,1)S(1)} %get-tuple-element.67.rest_1_), channel_id=1, source_target_pairs={{0,8},{4,12},{8,0},{12,4},{1,9},{5,13},{9,1},{13,5},{2,10},{6,14},... | collective-permute-start | bytes 688136 | tf_op jit(solution)/shard_map/ppermute | solution.py:24
  60.7 14.1 %collective-permute-start.8 = (bf16[896,128]{1,0:T(8,128)(2,1)S(1)}, bf16[896,128]{1,0:T(8,128)(2,1)S(1)}, u32[]{:S(2)}, u32[]{:S(2)}) collective-permute-start(bf16[896,128]{1,0:T(8,128)(2,1)S(1)} %pass_on.2), channel_id=1, source_target_pairs={{0,4},{4,0},{8,12},{12,8},{1,5},{5,1},{9,13},{13,9},{2,6},{6,2},{1... | collective-permute-start | bytes 688136 | tf_op jit(solution)/shard_map/ppermute | solution.py:24
  66.7 9.7 %collective-permute-start.13 = (bf16[896,128]{1,0:T(8,128)(2,1)S(1)}, bf16[896,128]{1,0:T(8,128)(2,1)S(1)}, u32[]{:S(2)}, u32[]{:S(2)}) collective-permute-start(bf16[896,128]{1,0:T(8,128)(2,1)S(1)} %pass_on.3), channel_id=1, source_target_pairs={{0,4},{4,0},{8,12},{12,8},{1,5},{5,1},{9,13},{13,9},{2,6},{6,2},{1... | collective-permute-start | bytes 688136 | tf_op jit(solution)/shard_map/ppermute | solution.py:24
